TPU v7x, 128 devices: a whole 4x4x4 slice. The times are simulated.
128 devices in a mesh: face: 8 (over z, x_lo), tile: 16 (over y, x_hi, core).
Axes of the slice: x: 4 (x_hi: 2, x_lo: 2; x = x_hi * 2 + x_lo), y: 4, z: 4, core: 2. Of those that a mesh axis runs over, the one named last changes fastest.
Arguments:
- atmosphere: float32 [192, 64, 4096], P(None, 'face', 'tile'), may hold values from -6 to 6
- ocean: float32 [96, 256, 2048], P(None, 'tile', 'face'), may hold values from -6 to 6
- kernel_atm: float32 [192, 49], replicated, may hold values from -0.875 to 0.875
- w_in_atm: float32 [192, 768], replicated, may hold values from -0.4375 to 0.4375
- w_out_atm: float32 [192, 768], replicated, may hold values from -0.21875 to 0.21875
- w_flux: float32 [64, 192], replicated, may hold values from -0.4375 to 0.4375
- kernel_ocean: float32 [96, 49], replicated, may hold values from -0.875 to 0.875
- w_in_ocean: float32 [96, 384], replicated, may hold values from -0.625 to 0.625
- w_out_ocean: float32 [96, 384], replicated, may hold values from -0.3125 to 0.3125
- w_couple: float32 [96, 64], replicated, may hold values from -0.75 to 0.75
- intersection_src: int32 [8, 512, 4], P('face', 'tile'), may hold values from 0 to 255, as said below
- intersection_count: int32 [8, 512], P('face', 'tile'), may hold values from 1 to 4
- intersection_weight: float32 [8, 512, 4, 128, 128], P('face', 'tile'), may hold values from -0.25 to 0.25
Outputs:
- atm_next: float32 [192, 64, 4096], P(None, 'face', 'tile')
- ocean_next: float32 [96, 256, 2048], P(None, 'tile', 'face')
Inputs may be any that keep to these rules, and one draw needn't show every extreme that they name: `intersection_src`: entries at slots k >= intersection_count are padding and name some block. Among the live pairs of the 32 ocean blocks of one device, at most 8 name blocks of one atmosphere tile, and in every device some tile is named by exactly 8 of them.
All inputs are finite; a program needn't handle non-finite values.
Results may differ from a plain program's by a relative error of at most 0.0003.
Values sent between devices are 32-bit elements; how exact they have to be, the bound alone decides.
A program may use at most 128 MiB of HBM per device.

v0:
```python
import jax
import jax.numpy as jnp
from jax import lax
from jax.sharding import PartitionSpec as P

HIGHEST = lax.Precision.HIGHEST


def padded_2(array, sides, width, wrap):
    for axis, dim in sides:
        count, length = (lax.axis_size(axis), array.shape[dim])
        up = [(i, (i + 1) % count) for i in range(count if wrap else count - 1)]
        down = [(j, i) for i, j in up]
        last = lax.slice_in_dim(array, length - width, length, axis=dim)
        initial = lax.slice_in_dim(array, 0, width, axis=dim)
        before = lax.ppermute(last, axis, up)
        after = lax.ppermute(initial, axis, down)
        array = jnp.concatenate([before, array, after], axis=dim)
    return array


def from_partner(value, axis, bit):
    mask = 2**bit
    pairs = [(source, source ^ mask) for source in range(lax.axis_size(axis))]
    return lax.ppermute(value, axis, pairs)


def depthwise(padded, kernel, row_count, col_count):
    running = jnp.zeros((padded.shape[0], row_count, col_count), jnp.float32)
    for shift_row in range(7):
        for shift_col in range(7):
            weight_here = kernel[:, shift_row * 7 + shift_col][:, None, None]
            running = (
                running
                + weight_here
                * padded[:, shift_row : shift_row + row_count, shift_col : shift_col + col_count]
            )
    return running


def normalize(values):
    average = jnp.mean(values, axis=0, keepdims=True)
    centred = values - average
    spread = jnp.mean(centred * centred, axis=0, keepdims=True)
    return centred * lax.rsqrt(spread + 1e-06)


def mixer(normed, w_in, w_out):
    hidden = jax.nn.gelu(
        jnp.einsum("ch,cxy->hxy", w_in, normed, precision=HIGHEST), approximate=False
    )
    return jnp.einsum("ch,hxy->cxy", w_out, hidden, precision=HIGHEST)


def body(
    atmosphere,
    ocean,
    kernel_atm,
    w_in_atm,
    w_out_atm,
    w_flux,
    kernel_ocean,
    w_in_ocean,
    w_out_ocean,
    w_couple,
    intersection_src,
    intersection_count,
    intersection_weight,
):
    rows_atm, cols_atm = (atmosphere.shape[1], atmosphere.shape[2])
    padded = padded_2(atmosphere, (("face", 1), ("tile", 2)), 3, True)
    filtered = depthwise(padded, kernel_atm, rows_atm, cols_atm)
    atm_next = atmosphere + mixer(normalize(filtered), w_in_atm, w_out_atm)
    latent = jnp.einsum("fc,cxy->fxy", w_flux, atm_next, precision=HIGHEST)
    latent_rows = latent.shape[0]
    block_width = intersection_weight.shape[-1]
    blocks_here = rows_atm * cols_atm // block_width
    flux_blocks = latent.reshape(latent_rows, blocks_here, block_width).transpose(1, 0, 2)
    lat_rows, lon_cols = (ocean.shape[1], ocean.shape[2])
    lon_pad = padded_2(ocean, (("face", 2),), 3, True)
    extended = padded_2(lon_pad, (("tile", 1),), 3, False)
    mirror = lon_pad[:, lat_rows - 3 :, :][:, ::-1, ::-1]
    for bit_index in range(lax.axis_size("face").bit_length() - 1):
        mirror = from_partner(mirror, "face", bit_index)
    northmost = lax.axis_index("tile") == lax.axis_size("tile") - 1
    northern = jnp.where(northmost, mirror, extended[:, lat_rows + 3 :, :])
    ocean_pad = jnp.concatenate([extended[:, : lat_rows + 3, :], northern], axis=1)
    filtered_sea = depthwise(ocean_pad, kernel_ocean, lat_rows, lon_cols)
    per_block = intersection_src.shape[2]
    dst_blocks = intersection_src.shape[1]
    pair_count = dst_blocks * per_block
    wanted_ids = intersection_src.reshape(pair_count)
    active = (
        jnp.arange(per_block, dtype=jnp.int32)[None, :]
        < intersection_count.reshape(dst_blocks)[:, None]
    )
    shard_rows = lax.all_gather(flux_blocks, "tile", axis=0, tiled=True)
    span = shard_rows.shape[0]
    inside = (wanted_ids >= 0) & (wanted_ids < span)
    fetched = shard_rows[jnp.clip(wanted_ids, 0, span - 1)]
    picked = jnp.where(
        inside[:, None, None],
        fetched,
        jnp.zeros((pair_count, latent_rows, block_width), jnp.float32),
    )
    selected = picked.reshape(dst_blocks, per_block, latent_rows, block_width)
    selected = jnp.where(active[:, :, None, None], selected, 0.0)
    regridded = jnp.einsum("pkfi,pkio->pfo", selected, intersection_weight[0], precision=HIGHEST)
    flux_grid = regridded.reshape(lat_rows, lon_cols // block_width, latent_rows, block_width)
    flux_grid = flux_grid.transpose(2, 0, 1, 3).reshape(latent_rows, lat_rows, lon_cols)
    mixed_in = normalize(filtered_sea) + jnp.einsum(
        "cf,fxy->cxy", w_couple, flux_grid, precision=HIGHEST
    )
    ocean_next = ocean + mixer(mixed_in, w_in_ocean, w_out_ocean)
    return (atm_next, ocean_next)


def solution(mesh):
    return jax.shard_map(
        body,
        mesh=mesh,
        in_specs=(
            P(None, "face", "tile"),
            P(None, "tile", "face"),
            P(),
            P(),
            P(),
            P(),
            P(),
            P(),
            P(),
            P(),
            P("face", "tile", None),
            P("face", "tile"),
            P("face", "tile", None, None, None),
        ),
        out_specs=(P(None, "face", "tile"), P(None, "tile", "face")),
        check_vma=False,
    )
```

profile of v0, /device:TPU:1, one launch (start us, length us, event | category | flops | bytes accessed | tf_op | source)
XLA Modules:
  0.0 323.7 jit_solution(3369482260894053088)
XLA Ops:
  10.4 5.5 %collective-permute-start.1 = (f32[192,3,256]{2,0,1:T(8,128)}, f32[192,3,256]{2,0,1:T(8,128)S(1)}, u32[]{:S(2)}, u32[]{:S(2)}) collective-permute-start(f32[192,3,256]{2,0,1:T(8,128)} %copy.89), channel_id=1, source_target_pairs={{16,0},{32,16},{48,32},{64,48},{80,64},{96,80},{112,96},{0,112},{1... | collective-permute-start | bytes 1769480 | tf_op jit(solution)/shard_map/ppermute | solution.py:17
  19.1 9.2 %collective-permute-done.1 = f32[192,3,256]{2,0,1:T(8,128)S(1)} collective-permute-done((f32[192,3,256]{2,0,1:T(8,128)}, f32[192,3,256]{2,0,1:T(8,128)S(1)}, u32[]{:S(2)}, u32[]{:S(2)}) %collective-permute-start.1) | collective-permute-done | bytes 589856 | tf_op jit(solution)/shard_map/ppermute | solution.py:17
  29.5 12.3 %collective-permute-done = f32[192,3,256]{2,0,1:T(8,128)} collective-permute-done((f32[192,3,256]{2,0,1:T(8,128)}, f32[192,3,256]{2,0,1:T(8,128)}, u32[]{:S(2)}, u32[]{:S(2)}) %collective-permute-start) | collective-permute-done | bytes 589856 | tf_op jit(solution)/shard_map/ppermute | solution.py:16
  41.9 2.4 copy.40
  45.2 4.2 %collective-permute-start.2 = (f32[192,14,3]{0,1,2:T(8,128)S(1)}, f32[192,14,3]{0,1,2:T(8,128)S(1)}, u32[]{:S(2)}, u32[]{:S(2)}) collective-permute-start(f32[192,14,3]{0,1,2:T(8,128)S(1)} %get-tuple-element.14), channel_id=1, source_target_pairs={{0,1},{1,2},{2,3},{3,4},{4,5},{5,6},{6,7},{7,8},{8,9},{9,10},{10,1... | collective-permute-start | bytes 96776 | tf_op jit(solution)/shard_map/ppermute | solution.py:16
  50.6 4.0 %collective-permute-done.3 = f32[192,14,3]{0,1,2:T(8,128)S(1)} collective-permute-done((f32[192,14,3]{0,1,2:T(8,128)S(1)}, f32[192,14,3]{0,1,2:T(8,128)S(1)}, u32[]{:S(2)}, u32[]{:S(2)}) %collective-permute-start.3) | collective-permute-done | bytes 32288 | tf_op jit(solution)/shard_map/ppermute | solution.py:17
  54.6 4.4 %maximum_maximum_fusion = (f32[192,14,259]{0,1,2:T(8,128)}, f32[192,14,259]{0,1,2:T(8,128)}) fusion(f32[192,3,256]{0,1,2:T(4,128)S(1)} %copy-done.4, f32[192,8,256]{0,1,2:T(8,128)S(1)} %copy.41, f32[192,3,256]{0,1,2:T(4,128)S(1)} %copy-done.5, f32[192,14,3]{0,1,2:T(8,128)S(1)} %collective-permute-done.2, f32[192,14,3]{0,1,2:T(8,128)S(1)} %collective-permute-done.3), kind=kLoop, calls=%fused_computation.141 | loop fusion | flops 4177152 | bytes 8386560 | tf_op jit(solution)/shard_map/concatenate | solution.py:18
  59.0 82.4 %fusion.398 = (f32[8,256]{0,1:T(8,128)S(1)}, f32[192,8,256]{0,1,2:T(8,128)}) fusion(f32[192,14,259]{0,1,2:T(8,128)} %get-tuple-element.13, f32[192]{0:T(256)S(1)} %bitcast.435, f32[192]{0:T(256)S(1)} %bitcast.436, f32[192]{0:T(256)S(1)} %bitcast.389, f32[192,3,256]{0,1,2:T(4,128)} %copy.42, f32[192,8,256]{0,1,2:T(8,128)S(1)} %copy.41, f32[192]{0:T(256)S(1)} %bitcast.390, ...), kind=kLoop, calls=%fused_computation.573 | loop fusion | flops 40892416 | bytes 70431488 | tf_op jit(solution)/shard_map/reduce_sum | solution.py:42
  141.4 2.4 multiply_reduce_fusion
  144.6 6.1 %fusion.254 = f32[8,256,768]{2,1,0:T(8,128)S(1)} fusion(f32[192,8,256]{0,1,2:T(8,128)S(1)} %subtract_multiply_fusion, f32[192,768]{1,0:T(8,128)S(1)} %copy-done), kind=kOutput, calls=%fused_computation.317 | convolution fusion | flops 3623878656 | bytes 8454144 | tf_op jit(solution)/shard_map/ch,cxy->hxy/dot_general | solution.py:50
  150.8 21.3 %bitcast_add_fusion.3 = f32[192,8,256]{2,0,1:T(8,128)S(1)} fusion(f32[8,256,768]{2,1,0:T(8,128)S(1)} %fusion.254, f32[192,768]{1,0:T(8,128)S(1)} %copy-done.19, f32[192,8,256]{2,1,0:T(8,128)S(1)} %copy-done.8), kind=kOutput, calls=%fused_computation.429 | convolution fusion | flops 3724935168 | bytes 10027008 | tf_op jit(solution)/shard_map/ch,hxy->cxy/dot_general | solution.py:52
  180.4 2.3 copy.74
  188.6 12.2 %collective-permute-done.7 = f32[96,3,262]{0,2,1:T(8,128)} collective-permute-done((f32[96,3,262]{0,2,1:T(8,128)S(1)}, f32[96,3,262]{0,2,1:T(8,128)}, u32[]{:S(2)}, u32[]{:S(2)}) %collective-permute-start.7) | collective-permute-done | bytes 301856 | tf_op jit(solution)/shard_map/ppermute | solution.py:25
  202.3 5.3 %collective-permute-start.6 = (f32[96,3,262]{0,2,1:T(8,128)S(1)}, f32[96,3,262]{0,2,1:T(8,128)S(1)}, u32[]{:S(2)}, u32[]{:S(2)}) collective-permute-start(f32[96,3,262]{0,2,1:T(8,128)S(1)} %copy.56), channel_id=1, source_target_pairs={{0,1},{1,2},{2,3},{3,4},{4,5},{5,6},{6,7},{7,8},{8,9},{9,10},{10,1... | collective-permute-start | bytes 905480 | tf_op jit(solution)/shard_map/ppermute | solution.py:16
  210.9 3.0 collective-permute-start.9
  214.9 5.6 %collective-permute-done.10 = f32[96,3,262]{0,2,1:T(8,128)S(1)} collective-permute-done((f32[96,3,262]{0,2,1:T(8,128)S(1)}, f32[96,3,262]{0,2,1:T(8,128)S(1)}, u32[]{:S(2)}, u32[]{:S(2)}) %collective-permute-start.10) | collective-permute-done | bytes 301856 | tf_op jit(solution)/shard_map/ppermute | solution.py:17
  220.8 3.5 %copy.75 = f32[192,8,256]{2,1,0:T(8,128)} copy(f32[192,8,256]{2,0,1:T(8,128)} %copy-done.11) | data formatting | bytes 3145728
  225.5 6.0 %maximum_maximum_fusion.1 = (f32[96,19,262]{2,0,1:T(8,128)S(1)}, f32[96,19,262]{2,0,1:T(8,128)}) fusion(f32[96,16,3]{2,0,1:T(8,128)} %copy-done.7, f32[96,16,256]{2,0,1:T(8,128)} %copy-done.2, f32[96,16,3]{2,0,1:T(8,128)} %copy.53, f32[96,3,262]{2,0,1:T(8,128)} %copy.57, f32[96,3,262]{2,0,1:T(8,128)S(1)} %broadcast_select_fusion), kind=kLoop, calls=%fused_computation.209 | loop fusion | flops 2867328 | bytes 6036480 | tf_op jit(solution)/shard_map/concatenate | solution.py:18
  231.5 32.4 %fusion.396 = (f32[16,256]{1,0:T(8,128)S(1)}, f32[96,16,256]{2,0,1:T(8,128)}) fusion(f32[96,19,262]{2,0,1:T(8,128)} %get-tuple-element.17, f32[96]{0:T(128)S(1)} %get-tuple-element.120, f32[96]{0:T(128)S(1)} %get-tuple-element.121, f32[96]{0:T(128)S(1)} %get-tuple-element.74, f32[96]{0:T(128)S(1)} %get-tuple-element.75, f32[96]{0:T(128)S(1)} %get-tuple-element.76, ...), kind=kLoop, calls=%fused_computation.572 | loop fusion | flops 40890368 | bytes 69278080 | tf_op jit(solution)/shard_map/reduce_sum | solution.py:42
  265.5 6.2 %gather_fusion = f32[128,64,128]{2,1,0:T(8,128)} fusion(f32[256,64,128]{2,1,0:T(8,128)} %all-gather.2.cloned.1.call-done, s32[1024]{0:T(1024)S(1)} %pad_clamp_fusion), kind=kCustom, calls=%fused_computation | custom fusion | bytes 8389120 | tf_op jit(solution)/shard_map/gather | solution.py:100
  271.7 9.1 %fusion = f32[32,64,128,1]{2,1,3,0:T(8,128)S(1)} fusion(f32[1,32,4,128,128]{4,3,2,1,0:T(8,128)} %param.25, f32[32,4,64,128]{3,2,1,0:T(8,128)} %bitcast.383, pred[32,4]{1,0:T(8,128)(4,1)S(1)} %copy.67, pred[32,4]{1,0:T(8,128)(4,1)S(1)} %iota_compare_fusion), kind=kOutput, calls=%fused_computation.3 | convolution fusion | flops 1612709888 | bytes 13631744 | tf_op jit(solution)/shard_map/pkfi,pkio->pfo/dot_general | solution.py:108
  283.5 3.2 fusion.324
  286.8 5.7 %fusion.317 = f32[16,256,384]{2,1,0:T(8,128)S(1)} fusion(f32[16,256,96]{1,2,0:T(8,128)S(1)} %fusion.324, f32[96,16,256]{2,0,1:T(8,128)S(1)} %copy-done.6, f32[16,256]{1,0:T(8,128)S(1)} %add_rsqrt_fusion.1, f32[16,256]{1,0:T(8,128)S(1)} %broadcast_multiply_fusion.1, f32[96,384]{1,0:T(8,128)S(1)} %copy-done.12), kind=kOutput, calls=%fused_computation.428 | convolution fusion | flops 1813118976 | bytes 9617408 | tf_op jit(solution)/shard_map/ch,cxy->hxy/dot_general | solution.py:50
  292.5 22.1 %bitcast_add_fusion = f32[96,16,256]{2,0,1:T(8,128)S(1)} fusion(f32[16,256,384]{2,1,0:T(8,128)S(1)} %fusion.317, f32[96,384]{1,0:T(8,128)S(1)} %copy-done.20, f32[96,16,256]{2,1,0:T(8,128)S(1)} %copy-done.10), kind=kOutput, calls=%fused_computation.426 | convolution fusion | flops 1912995840 | bytes 9584640 | tf_op jit(solution)/shard_map/ch,hxy->cxy/dot_general | solution.py:52
  (106 shorter events, 38.1 us)
Async XLA Ops:
  7.2 137.5 %copy-start = (f32[192,768]{1,0:T(8,128)S(1)}, f32[192,768]{1,0:T(8,128)}, u32[]{:S(2)}) copy-start(f32[192,768]{1,0:T(8,128)} %param.16) | copy-start | bytes 1769476
  7.2 258.3 %all-gather.2.cloned.1.call-start = ((), (), s32[]{:S(2)}) async-start(), calls=%async_computation | async-start | bytes 8912896 | tf_op jit(solution)/shard_map/all_gather | solution.py:97
  10.4 17.8 %collective-permute-start.1 = (f32[192,3,256]{2,0,1:T(8,128)}, f32[192,3,256]{2,0,1:T(8,128)S(1)}, u32[]{:S(2)}, u32[]{:S(2)}) collective-permute-start(f32[192,3,256]{2,0,1:T(8,128)} %copy.89), channel_id=1, source_target_pairs={{16,0},{32,16},{48,32},{64,48},{80,64},{96,80},{112,96},{0,112},{1... | collective-permute-start | bytes 1769480 | tf_op jit(solution)/shard_map/ppermute | solution.py:17
  16.8 25.0 %collective-permute-start = (f32[192,3,256]{2,0,1:T(8,128)}, f32[192,3,256]{2,0,1:T(8,128)}, u32[]{:S(2)}, u32[]{:S(2)}) collective-permute-start(f32[192,3,256]{2,0,1:T(8,128)} %copy.90), channel_id=1, source_target_pairs={{0,16},{16,32},{32,48},{48,64},{64,80},{80,96},{96,112},{112,0},{1... | collective-permute-start | bytes 1769480 | tf_op jit(solution)/shard_map/ppermute | solution.py:16
  44.2 10.4 %copy-start.4 = (f32[192,3,256]{0,1,2:T(4,128)S(1)}, f32[192,3,256]{0,1,2:T(4,128)}, u32[]{:S(2)}) copy-start(f32[192,3,256]{0,1,2:T(4,128)} %copy.42) | copy-start | bytes 1769476
  44.2 10.4 %copy-start.5 = (f32[192,3,256]{0,1,2:T(4,128)S(1)}, f32[192,3,256]{0,1,2:T(4,128)}, u32[]{:S(2)}) copy-start(f32[192,3,256]{0,1,2:T(4,128)} %copy.40) | copy-start | bytes 1769476
  45.2 5.4 %collective-permute-start.2 = (f32[192,14,3]{0,1,2:T(8,128)S(1)}, f32[192,14,3]{0,1,2:T(8,128)S(1)}, u32[]{:S(2)}, u32[]{:S(2)}) collective-permute-start(f32[192,14,3]{0,1,2:T(8,128)S(1)} %get-tuple-element.14), channel_id=1, source_target_pairs={{0,1},{1,2},{2,3},{3,4},{4,5},{5,6},{6,7},{7,8},{8,9},{9,10},{10,1... | collective-permute-start | bytes 96776 | tf_op jit(solution)/shard_map/ppermute | solution.py:16
  49.4 5.2 %collective-permute-start.3 = (f32[192,14,3]{0,1,2:T(8,128)S(1)}, f32[192,14,3]{0,1,2:T(8,128)S(1)}, u32[]{:S(2)}, u32[]{:S(2)}) collective-permute-start(f32[192,14,3]{0,1,2:T(8,128)S(1)} %get-tuple-element.15), channel_id=1, source_target_pairs={{1,0},{2,1},{3,2},{4,3},{5,4},{6,5},{7,6},{8,7},{9,8},{10,9},{11,1... | collective-permute-start | bytes 96776 | tf_op jit(solution)/shard_map/ppermute | solution.py:17
  144.6 6.2 %copy-start.8 = (f32[192,8,256]{2,1,0:T(8,128)S(1)}, f32[192,8,256]{2,1,0:T(8,128)}, u32[]{:S(2)}) copy-start(f32[192,8,256]{2,1,0:T(8,128)} %param.13) | copy-start | bytes 4718596
  144.6 6.2 %copy-start.19 = (f32[192,768]{1,0:T(8,128)S(1)}, f32[192,768]{1,0:T(8,128)}, u32[]{:S(2)}) copy-start(f32[192,768]{1,0:T(8,128)} %param.17) | copy-start | bytes 1769476
  150.8 22.5 %copy-start.13 = (f32[64,192]{1,0:T(8,128)S(1)}, f32[64,192]{1,0:T(8,128)}, u32[]{:S(2)}) copy-start(f32[64,192]{1,0:T(8,128)} %param.18) | copy-start | bytes 147460
  178.5 4.3 %collective-permute-start.5 = (f32[96,16,3]{0,1,2:T(8,128)S(1)}, f32[96,16,3]{0,1,2:T(8,128)S(1)}, u32[]{:S(2)}, u32[]{:S(2)}) collective-permute-start(f32[96,16,3]{0,1,2:T(8,128)S(1)} %copy.81), channel_id=1, source_target_pairs={{16,0},{32,16},{48,32},{64,48},{80,64},{96,80},{112,96},{0,112},{1... | collective-permute-start | bytes 55304 | tf_op jit(solution)/shard_map/ppermute | solution.py:17
  179.0 4.8 %collective-permute-start.4 = (f32[96,16,3]{0,1,2:T(8,128)S(1)}, f32[96,16,3]{0,1,2:T(8,128)S(1)}, u32[]{:S(2)}, u32[]{:S(2)}) collective-permute-start(f32[96,16,3]{0,1,2:T(8,128)S(1)} %copy.80), channel_id=1, source_target_pairs={{0,16},{16,32},{32,48},{48,64},{64,80},{80,96},{96,112},{112,0},{1... | collective-permute-start | bytes 55304 | tf_op jit(solution)/shard_map/ppermute | solution.py:16
  182.8 41.5 %copy-start.2 = (f32[96,16,256]{2,0,1:T(8,128)}, f32[96,16,256]{2,0,1:T(8,128)S(1)}, u32[]{:S(2)}) copy-start(f32[96,16,256]{2,0,1:T(8,128)S(1)} %copy.74) | copy-start | bytes 4718596
  187.6 13.2 %collective-permute-start.7 = (f32[96,3,262]{0,2,1:T(8,128)S(1)}, f32[96,3,262]{0,2,1:T(8,128)}, u32[]{:S(2)}, u32[]{:S(2)}) collective-permute-start(f32[96,3,262]{0,2,1:T(8,128)S(1)} %copy.63), channel_id=1, source_target_pairs={{0,16},{16,0},{32,48},{48,32},{64,80},{80,64},{96,112},{112,96},{1... | collective-permute-start | bytes 905480 | tf_op jit(solution)/shard_map/ppermute | solution.py:25
  200.8 10.1 %collective-permute-start.8 = (f32[96,3,262]{0,2,1:T(8,128)}, f32[96,3,262]{0,2,1:T(8,128)}, u32[]{:S(2)}, u32[]{:S(2)}) collective-permute-start(f32[96,3,262]{0,2,1:T(8,128)} %collective-permute-done.7), channel_id=1, source_target_pairs={{0,32},{16,48},{32,0},{48,16},{64,96},{80,112},{96,64},{112,80},{1... | collective-permute-start | bytes 905480 | tf_op jit(solution)/shard_map/ppermute | solution.py:25
  202.3 11.6 %collective-permute-start.6 = (f32[96,3,262]{0,2,1:T(8,128)S(1)}, f32[96,3,262]{0,2,1:T(8,128)S(1)}, u32[]{:S(2)}, u32[]{:S(2)}) collective-permute-start(f32[96,3,262]{0,2,1:T(8,128)S(1)} %copy.56), channel_id=1, source_target_pairs={{0,1},{1,2},{2,3},{3,4},{4,5},{5,6},{6,7},{7,8},{8,9},{9,10},{10,1... | collective-permute-start | bytes 905480 | tf_op jit(solution)/shard_map/ppermute | solution.py:16
  207.9 12.7 %collective-permute-start.10 = (f32[96,3,262]{0,2,1:T(8,128)S(1)}, f32[96,3,262]{0,2,1:T(8,128)S(1)}, u32[]{:S(2)}, u32[]{:S(2)}) collective-permute-start(f32[96,3,262]{0,2,1:T(8,128)S(1)} %copy.64), channel_id=1, source_target_pairs={{1,0},{2,1},{3,2},{4,3},{5,4},{6,5},{7,6},{8,7},{9,8},{10,9},{11,1... | collective-permute-start | bytes 905480 | tf_op jit(solution)/shard_map/ppermute | solution.py:17
  210.9 13.4 %collective-permute-start.9 = (f32[96,3,262]{0,2,1:T(8,128)}, f32[96,3,262]{0,2,1:T(8,128)}, u32[]{:S(2)}, u32[]{:S(2)}) collective-permute-start(f32[96,3,262]{0,2,1:T(8,128)} %collective-permute-done.8), channel_id=1, source_target_pairs={{0,64},{16,80},{32,96},{48,112},{64,0},{80,16},{96,32},{112,48},{1... | collective-permute-start | bytes 905480 | tf_op jit(solution)/shard_map/ppermute | solution.py:25
  281.7 5.1 %copy-start.6 = (f32[96,16,256]{2,0,1:T(8,128)S(1)}, f32[96,16,256]{2,0,1:T(8,128)}, u32[]{:S(2)}) copy-start(f32[96,16,256]{2,0,1:T(8,128)} %get-tuple-element.9) | copy-start | bytes 4718596
  281.7 5.1 %copy-start.12 = (f32[96,384]{1,0:T(8,128)S(1)}, f32[96,384]{1,0:T(8,128)}, u32[]{:S(2)}) copy-start(f32[96,384]{1,0:T(8,128)} %param.20) | copy-start | bytes 442372
  286.8 5.7 %copy-start.10 = (f32[96,16,256]{2,1,0:T(8,128)S(1)}, f32[96,16,256]{2,1,0:T(8,128)}, u32[]{:S(2)}) copy-start(f32[96,16,256]{2,1,0:T(8,128)} %param.14) | copy-start | bytes 4718596
  286.8 5.7 %copy-start.20 = (f32[96,384]{1,0:T(8,128)S(1)}, f32[96,384]{1,0:T(8,128)}, u32[]{:S(2)}) copy-start(f32[96,384]{1,0:T(8,128)} %param.21) | copy-start | bytes 442372
  292.5 24.1 %copy-start.1 = (f32[192,768]{1,0:T(8,128)S(1)}, f32[192,768]{1,0:T(8,128)}, u32[]{:S(2)}) copy-start(f32[192,768]{1,0:T(8,128)} %param.16) | copy-start | bytes 1769476
  (9 other events, 24.3 us)
Sparse Core Ops, SparseCore 0:
  175.9 77.2 all-gather.1
where the time goes:
time: 328 us; the launch traced here: 324 us
  other arithmetic  132 us (40%)
  matrix products  68.7 us (21%)
  waiting for transfers between devices  46.1 us (14%)
  local copies, waits for them, and re-layouts  38 us (12%)
  starting transfers between devices  23.7 us (7%)
  between operations  14.7 us (4%)
    reduce_sum x2, other arithmetic, normalize(): average = jnp.mean(values, axis=0, keepdims=True)  115 us
    dot_general x2, matrix products, mixer(): return jnp.einsum('ch,hxy->cxy', w_out, hidden, precision=HIGHEST)  43.4 us
    ppermute x4, waiting for transfers between devices, padded_2(): after = lax.ppermute(initial, axis, down)  18.8 us
    unnamed x52, local copies, waits for them, and re-layouts  15.9 us
    ppermute x4, waiting for transfers between devices, padded_2(): before = lax.ppermute(last, axis, up)  14 us
    ppermute x3, waiting for transfers between devices, from_partner(): return lax.ppermute(value, axis, pairs)  13.3 us
    dot_general x2, matrix products, mixer(): jnp.einsum('ch,cxy->hxy', w_in, normed, precision=HIGHEST)  11.9 us
    concatenate x3, other arithmetic, padded_2(): array = jnp.concatenate([before, array, after], axis=dim)  11.8 us
  transfers between devices with their start and end apart: 12, of which 8 were waited for; matrix products, arithmetic and copies ran while one was open for 19% of the time, Pallas kernels for 0%

commit v1 on v0

v1 whole, which is shorter than its diff:
```python
import functools

import jax
import jax.numpy as jnp
from jax import lax
from jax.experimental import pallas as pl
from jax.experimental.pallas import tpu as pltpu
from jax.sharding import PartitionSpec as P

F32 = jnp.float32
BF16 = jnp.bfloat16
MESH = pl.DeviceIdType.MESH
MIB = 2**20
VMEM = pl.BlockSpec(memory_space=pltpu.VMEM)
SMEM = pl.BlockSpec(memory_space=pltpu.SMEM)
ANY = pl.BlockSpec(memory_space=pl.ANY)
DMA = pltpu.SemaphoreType.DMA

CA, HA, CO, HO, FL = 192, 768, 96, 384, 64
AR, OR, COLS = 8, 16, 256
N_FACE, N_TILE = 8, 16


def split(x):
    hi = x.astype(BF16)
    return hi, (x - hi.astype(F32)).astype(BF16)


def mm(a, b):
    return jnp.dot(a, b, preferred_element_type=F32)


def mm3(a, b):
    return mm(a[0], b[0]) + (mm(a[1], b[0]) + mm(a[0], b[1]))


def gelu(x):
    return 0.5 * x * (1.0 + lax.erf(x * 0.7071067811865476))


def layer_norm(v):
    centred = v - jnp.mean(v, axis=0, keepdims=True)
    spread = jnp.mean(centred * centred, axis=0, keepdims=True)
    return centred * lax.rsqrt(spread + 1e-06)


def lanes():
    return lax.broadcasted_iota(jnp.int32, (8, 128), 1)


def group(g):
    return pl.ds(pl.multiple_of(g * 8, 8), 8)


def rows_out_of(raw, rows, channels, wide):
    for half in range(2):
        flat = raw.at[half].reshape(channels * rows, 128)
        for r in range(rows):
            wide[r, :, half * 128 : half * 128 + 128] = flat[pl.ds(r, channels, stride=rows), :]


def pack_edges(wide, first, rows, right, left):
    span = 4 * rows
    slots = 128 // span

    def step(v, carry):
        lane = lanes()
        to_right = jnp.zeros((8, 128), F32)
        to_left = jnp.zeros((8, 128), F32)
        for s in range(slots):
            here = group(v * slots + s)
            for r in range(rows):
                at = s * span + 4 * r
                mask = (lane >= at) & (lane < at + 3)
                last = wide[first + r, here, 128:256]
                initial = wide[first + r, here, 0:128]
                to_right = jnp.where(mask, pltpu.roll(last, (at - 125) % 128, 1), to_right)
                to_left = jnp.where(mask, pltpu.roll(initial, at, 1) if at else initial, to_left)
        right[group(v), :] = to_right
        left[group(v), :] = to_left
        return carry

    lax.fori_loop(0, 6, step, 0)


def unpack_edges(pairs, rows, halo):
    span = 4 * rows
    slots = 128 // span

    def step(v, carry):
        lane = lanes()
        for s in range(slots):
            here = group(v * slots + s)
            for target, source, from_left, from_right in pairs:
                at = s * span + 4 * source
                after = from_right[group(v), :]
                before = from_left[group(v), :]
                after = pltpu.roll(after, (128 - at) % 128, 1) if at else after
                before = pltpu.roll(before, (125 - at) % 128, 1)
                halo[target, here, :] = jnp.where(lane < 3, after, jnp.where(lane >= 125, before, 0.0))
        return carry

    lax.fori_loop(0, 6, step, 0)


def spread_taps(kernel_ref, channels, table):
    kernel = jnp.transpose(kernel_ref[...])
    for tap in range(49):
        table[tap] = jnp.broadcast_to(kernel[:, tap : tap + 1], (channels, 128))


def depthwise(wide, halo, table, channels, tops, base, out):
    needed = sorted({t + i for t in tops for i in range(7)})

    def step(g, carry):
        here = group(g)
        lane = lanes()
        sums = [[jnp.zeros((8, 128), F32)] * 2 for _ in tops]
        for j in range(7):
            shift = j - 3
            weights = [table[i * 7 + j, here, :] for i in range(7)]
            for row in needed:
                a = wide[base + row, here, 0:128]
                b = wide[base + row, here, 128:256]
                if shift > 0:
                    keep = lane < 128 - shift
                    c = pltpu.roll(halo[base + row, here, :], 128 - shift, 1)
                    a = pltpu.roll(a, 128 - shift, 1)
                    b = pltpu.roll(b, 128 - shift, 1)
                    a, b = jnp.where(keep, a, b), jnp.where(keep, b, c)
                elif shift < 0:
                    keep = lane >= -shift
                    c = pltpu.roll(halo[base + row, here, :], -shift, 1)
                    a = pltpu.roll(a, -shift, 1)
                    b = pltpu.roll(b, -shift, 1)
                    a, b = jnp.where(keep, a, c), jnp.where(keep, b, a)
                for n, t in enumerate(tops):
                    i = row - t
                    if 0 <= i < 7:
                        sums[n] = [sums[n][0] + weights[i] * a, sums[n][1] + weights[i] * b]
        for n in range(len(tops)):
            out[n, here, 0:128] = sums[n][0]
            out[n, here, 128:256] = sums[n][1]
        return carry

    lax.fori_loop(0, channels // 8, step, 0)


def mixer(normed, w_in, w_out, hidden, chunk=256):
    size = w_in[0].shape[0]
    for start in range(0, size, chunk):
        part = pl.ds(start, min(chunk, size - start))
        value = gelu(mm3((w_in[0][part, :], w_in[1][part, :]), normed))
        hidden[0][part, :], hidden[1][part, :] = split(value)
    return mm3((w_out[0][...], w_out[1][...]), (hidden[0][...], hidden[1][...]))


def position():
    face = lax.axis_index("face")
    tile = lax.axis_index("tile")
    return face, tile


def ring(value, step, count):
    return lax.rem(value + (step + count), count)


def halo_kernel(
    atm_hbm, sea_hbm, aw, ah, sw, sh,
    atm_raw, sea_raw, a_out, a_in, s_out, s_in, mirror_w, mirror_h,
    load_sem, send_sem, recv_sem,
):
    face, tile = position()
    up, down = ring(face, 1, N_FACE), ring(face, -1, N_FACE)
    north, south = ring(tile, 1, N_TILE), ring(tile, -1, N_TILE)
    loads = []
    for half in range(2):
        cut = pl.ds(128 * half, 128)
        loads.append(pltpu.make_async_copy(atm_hbm.at[:, :, cut], atm_raw.at[half], load_sem.at[half]))
        loads.append(pltpu.make_async_copy(sea_hbm.at[:, :, cut], sea_raw.at[half], load_sem.at[2 + half]))
    for load in loads:
        load.start()
    barrier = pltpu.get_barrier_semaphore()
    near = [
        (up, tile), (down, tile), (face, north), (face, south),
        (up, north), (up, south), (down, north), (down, south),
    ]
    for device in near:
        pl.semaphore_signal(barrier, inc=1, device_id=device, device_id_type=MESH)
    top = tile == N_TILE - 1
    across = (N_FACE - 1 - face, tile)

    @pl.when(top)
    def _():
        pl.semaphore_signal(barrier, inc=1, device_id=across, device_id_type=MESH)

    pl.semaphore_wait(barrier, len(near) + tile // (N_TILE - 1))

    def copy(k, src, dst, device):
        return pltpu.make_async_remote_copy(
            src_ref=src, dst_ref=dst, send_sem=send_sem.at[k], recv_sem=recv_sem.at[k],
            device_id=device, device_id_type=MESH,
        )

    loads[0].wait()
    loads[2].wait()
    rows_out_of(atm_raw, AR, CA, aw.at[pl.ds(3, AR)])
    copies = []
    for d in range(3):
        copies.append(copy(2 * d, aw.at[10 - d], aw.at[2 - d], (up, tile)))
        copies.append(copy(2 * d + 1, aw.at[3 + d], aw.at[11 + d], (down, tile)))
    for c in copies:
        c.start()
    pack_edges(aw, 3, AR, a_out.at[0], a_out.at[1])
    for n, f in enumerate((up, face, down)):
        copies.append(copy(6 + n, a_out.at[0], a_in.at[0, n], (f, north)))
        copies.append(copy(9 + n, a_out.at[1], a_in.at[1, n], (f, south)))
    for c in copies[6:]:
        c.start()
    loads[1].wait()
    loads[3].wait()
    rows_out_of(sea_raw, OR, CO, sw.at[pl.ds(3, OR)])
    first = len(copies)
    copies.append(copy(12, sw.at[pl.ds(16, 3)], sw.at[pl.ds(0, 3)], (face, north)))
    copies.append(copy(13, sw.at[pl.ds(3, 3)], sw.at[pl.ds(19, 3)], (face, south)))
    for c in copies[first:]:
        c.start()
    pack_edges(sw, 3, OR, s_out.at[0], s_out.at[1])
    first = len(copies)
    for n, t in enumerate((north, tile, south)):
        copies.append(copy(14 + n, s_out.at[0], s_in.at[0, n], (up, t)))
        copies.append(copy(17 + n, s_out.at[1], s_in.at[1, n], (down, t)))
    for c in copies[first:]:
        c.start()
    for c in copies[6:12]:
        c.wait()
    rows = [(r, AR - 3 + r, a_in.at[0, 0], a_in.at[1, 0]) for r in range(3)]
    rows += [(3 + r, r, a_in.at[0, 1], a_in.at[1, 1]) for r in range(AR)]
    rows += [(3 + AR + r, r, a_in.at[0, 2], a_in.at[1, 2]) for r in range(3)]
    unpack_edges(rows, AR, ah)
    for c in copies[12:]:
        c.wait()
    rows = [(r, OR - 3 + r, s_in.at[0, 0], s_in.at[1, 0]) for r in range(3)]
    rows += [(3 + r, r, s_in.at[0, 1], s_in.at[1, 1]) for r in range(OR)]
    rows += [(3 + OR + r, r, s_in.at[0, 2], s_in.at[1, 2]) for r in range(3)]
    unpack_edges(rows, OR, sh)

    @pl.when(tile == 0)
    def _():
        sw[0:3] = jnp.zeros((3, CO, COLS), F32)
        sh[0:3] = jnp.zeros((3, CO, 128), F32)

    @pl.when(top)
    def _():
        fold = [
            copy(20, sw.at[pl.ds(16, 3)], mirror_w, across),
            copy(21, sh.at[pl.ds(16, 3)], mirror_h, across),
        ]
        for c in fold:
            c.start()
        for c in fold:
            c.wait()
        flip = 127 - lax.broadcasted_iota(jnp.int32, (CO, 128), 1)
        for k in range(3):
            sw[19 + k, :, 0:128] = jnp.take_along_axis(mirror_w[2 - k, :, 128:256], flip, axis=1)
            sw[19 + k, :, 128:256] = jnp.take_along_axis(mirror_w[2 - k, :, 0:128], flip, axis=1)
            sh[19 + k] = jnp.take_along_axis(mirror_h[2 - k], flip, axis=1)

    for c in copies[:6]:
        c.wait()


def exchange(atmosphere, ocean):
    return pl.pallas_call(
        halo_kernel,
        out_shape=(
            jax.ShapeDtypeStruct((AR + 6, CA, COLS), F32),
            jax.ShapeDtypeStruct((AR + 6, CA, 128), F32),
            jax.ShapeDtypeStruct((OR + 6, CO, COLS), F32),
            jax.ShapeDtypeStruct((OR + 6, CO, 128), F32),
        ),
        in_specs=[ANY, ANY],
        out_specs=(VMEM,) * 4,
        scratch_shapes=[
            pltpu.VMEM((2, CA, AR, 128), F32),
            pltpu.VMEM((2, CO, OR, 128), F32),
            pltpu.VMEM((2, 48, 128), F32),
            pltpu.VMEM((2, 3, 48, 128), F32),
            pltpu.VMEM((2, 48, 128), F32),
            pltpu.VMEM((2, 3, 48, 128), F32),
            pltpu.VMEM((3, CO, COLS), F32),
            pltpu.VMEM((3, CO, 128), F32),
            DMA((4,)),
            DMA((22,)),
            DMA((22,)),
        ],
        compiler_params=pltpu.CompilerParams(
            collective_id=0, has_side_effects=True, vmem_limit_bytes=50 * MIB
        ),
        name="halo",
    )(atmosphere, ocean)


def place(row):
    return (3 - row) * 4 if row < 4 else (row - 4) * 4 + 2


def atm_kernel(
    aw, ah, kernel_ref, w_in_ref, w_out_ref, w_flux_ref, out, lat,
    table, conv, wi, wo, wf, normed, hidden, back,
):
    spread_taps(kernel_ref, CA, table)
    wi[0], wi[1] = split(jnp.transpose(w_in_ref[...]))
    wo[0], wo[1] = split(w_out_ref[...])
    wf[0], wf[1] = split(w_flux_ref[...])
    for stage in range(4):
        tops = (3 - stage, 4 + stage)
        depthwise(aw, ah, table, CA, tops, 0, conv)
        for n in range(2):
            cut = slice(n * COLS, n * COLS + COLS)
            normed[0, :, cut], normed[1, :, cut] = split(layer_norm(conv[n]))
        mixed = mixer(
            (normed[0], normed[1]), (wi.at[0], wi.at[1]), (wo.at[0], wo.at[1]),
            (hidden.at[0], hidden.at[1]),
        )
        for n, row in enumerate(tops):
            value = aw[3 + row] + mixed[:, n * COLS : n * COLS + COLS]
            flux = mm3((wf[0], wf[1]), split(value))
            for half in range(2):
                cut = slice(half * 128, half * 128 + 128)
                lat[place(row) + half] = flux[:, cut]
                back.at[half].reshape(CA * AR, 128)[pl.ds(row, CA, stride=AR), :] = value[:, cut]
    for half in range(2):
        out[:, :, half * 128 : half * 128 + 128] = back[half]


def atm_step(aw, ah, kernel_atm, w_in, w_out, w_flux):
    return pl.pallas_call(
        atm_kernel,
        out_shape=(
            jax.ShapeDtypeStruct((CA, AR, COLS), F32),
            jax.ShapeDtypeStruct((16, FL, 128), F32),
        ),
        in_specs=[VMEM] * 6,
        out_specs=(VMEM,) * 2,
        scratch_shapes=[
            pltpu.VMEM((49, CA, 128), F32),
            pltpu.VMEM((2, CA, COLS), F32),
            pltpu.VMEM((2, HA, CA), BF16),
            pltpu.VMEM((2, CA, HA), BF16),
            pltpu.VMEM((2, FL, CA), BF16),
            pltpu.VMEM((2, CA, 2 * COLS), BF16),
            pltpu.VMEM((2, HA, 2 * COLS), BF16),
            pltpu.VMEM((2, CA, AR, 128), F32),
        ],
        compiler_params=pltpu.CompilerParams(vmem_limit_bytes=50 * MIB),
        name="atmosphere",
    )(aw, ah, kernel_atm, w_in, w_out, w_flux)


def gather_kernel(lat, out, send_sem, recv_sem):
    face, tile = position()
    y, x, core = tile // 4, lax.rem(tile // 2, 2), lax.rem(tile, 2)

    def at(dy, dx, dc):
        return (ring(y, dy, 4) * 2 + lax.rem(x + dx, 2)) * 2 + lax.rem(core + dc, 2)

    targets = [at(0, 1, 0), at(1, 0, 0), at(-1, 0, 0), at(2, 0, 0), at(0, 0, 1)]
    barrier = pltpu.get_barrier_semaphore()
    for target in targets:
        pl.semaphore_signal(barrier, inc=1, device_id=(face, target), device_id_type=MESH)
    pl.semaphore_wait(barrier, len(targets))
    out[tile] = lat[...]

    def copy(stage, kind, block, target):
        part = out.at[block, pl.ds(4 * stage, 4)]
        return pltpu.make_async_remote_copy(
            src_ref=part, dst_ref=part, send_sem=send_sem.at[stage, kind], recv_sem=recv_sem.at[stage, kind],
            device_id=(face, target), device_id_type=MESH,
        )

    partner = at(0, 1, 0)
    steps = ((1, 1), (2, -1), (3, 2))
    sends = []
    for stage in range(4):
        mine = [copy(stage, 0, tile, partner)]
        mine += [copy(stage, kind, tile, at(dy, 0, 0)) for kind, dy in steps]
        mine += [copy(stage, 7, tile, at(0, 0, 1))]
        for c in mine:
            c.start()
        sends += mine
    for stage in range(4):
        copy(stage, 0, partner, partner).wait_recv()
        mine = [copy(stage, kind + 3, partner, at(dy, 0, 0)) for kind, dy in steps]
        mine += [copy(stage, 8, partner, at(0, 0, 1))]
        for c in mine:
            c.start()
        sends += mine
    for stage in range(4):
        for hop in range(2):
            for kind, dy in steps:
                block = at(-dy, hop, 0)
                copy(stage, kind + 3 * hop, block, partner).wait_recv()
                c = copy(stage, 8 + kind + 3 * hop, block, at(0, 0, 1))
                c.start()
                sends.append(c)
    for stage in range(4):
        copy(stage, 7, at(0, 0, 1), partner).wait_recv()
        copy(stage, 8, at(0, 1, 1), partner).wait_recv()
        for hop in range(2):
            for kind, dy in steps:
                copy(stage, 8 + kind + 3 * hop, at(-dy, hop, 1), partner).wait_recv()
    for c in sends:
        c.wait_send()


def gather(lat):
    return pl.pallas_call(
        gather_kernel,
        out_shape=jax.ShapeDtypeStruct((N_TILE, 16, FL, 128), F32),
        in_specs=[VMEM],
        out_specs=VMEM,
        scratch_shapes=[DMA((4, 15)), DMA((4, 15))],
        compiler_params=pltpu.CompilerParams(
            collective_id=1, has_side_effects=True, vmem_limit_bytes=50 * MIB
        ),
        name="gather",
    )(lat)


def ocean_kernel(
    src, count, sw, sh, blocks, weights, kernel_ref, w_in_ref, w_out_ref, w_couple_ref, out,
    table, conv, wi, wo, wc, normed, hidden, back,
):
    step = pl.program_id(0)

    @pl.when(step == 0)
    def _():
        spread_taps(kernel_ref, CO, table)
        wi[0], wi[1] = split(jnp.transpose(w_in_ref[...]))
        wo[0], wo[1] = split(w_out_ref[...])
        wc[0], wc[1] = split(jnp.transpose(w_couple_ref[...]))

    base = 2 * step
    depthwise(sw, sh, table, CO, (0, 1), base, conv)
    for n in range(2):
        for half in range(2):
            local = 2 * n + half
            block = 4 * step + local
            live = count[block]
            picked = []
            for k in range(4):
                index = src[k, block]
                t, a = index // 16, lax.rem(index, 16)
                r = a // 2
                spot = jnp.where(r < 4, (3 - r) * 4, (r - 4) * 4 + 2) + lax.rem(a, 2)
                picked.append(jnp.where(k < live, blocks[t, spot], 0.0))
            left = split(jnp.concatenate(picked, axis=1))
            right = split(weights[local].reshape(512, 128))
            flux = mm3(left, right)
            cut = slice(n * COLS + half * 128, n * COLS + half * 128 + 128)
            coupled = mm3((wc[0], wc[1]), split(flux))
            value = layer_norm(conv[n, :, half * 128 : half * 128 + 128]) + coupled
            normed[0, :, cut], normed[1, :, cut] = split(value)
    mixed = mixer(
        (normed[0], normed[1]), (wi.at[0], wi.at[1]), (wo.at[0], wo.at[1]),
        (hidden.at[0], hidden.at[1]), 128,
    )
    for n in range(2):
        value = sw[base + 3 + n] + mixed[:, n * COLS : n * COLS + COLS]
        for half in range(2):
            flat = back.at[half].reshape(CO * OR, 128)
            flat[pl.ds(base + n, CO, stride=OR), :] = value[:, half * 128 : half * 128 + 128]

    @pl.when(step == OR // 2 - 1)
    def _():
        for half in range(2):
            out[:, :, half * 128 : half * 128 + 128] = back[half]


def ocean_step(src, count, sw, sh, blocks, weights, kernel_ocean, w_in, w_out, w_couple):
    whole = lambda *shape: pl.BlockSpec(shape, lambda i: (0,) * len(shape))
    return pl.pallas_call(
        ocean_kernel,
        grid=(OR // 2,),
        out_shape=jax.ShapeDtypeStruct((CO, OR, COLS), F32),
        in_specs=[
            SMEM, SMEM,
            whole(OR + 6, CO, COLS), whole(OR + 6, CO, 128), whole(N_TILE, 16, FL, 128),
            pl.BlockSpec((4, 4, 128, 128), lambda i: (i, 0, 0, 0)),
            whole(49, CO), whole(CO, HO), whole(CO, HO), whole(FL, CO),
        ],
        out_specs=whole(CO, OR, COLS),
        scratch_shapes=[
            pltpu.VMEM((49, CO, 128), F32),
            pltpu.VMEM((2, CO, COLS), F32),
            pltpu.VMEM((2, HO, CO), BF16),
            pltpu.VMEM((2, CO, HO), BF16),
            pltpu.VMEM((2, CO, FL), BF16),
            pltpu.VMEM((2, CO, 2 * COLS), BF16),
            pltpu.VMEM((2, HO, 2 * COLS), BF16),
            pltpu.VMEM((2, CO, OR, 128), F32),
        ],
        compiler_params=pltpu.CompilerParams(vmem_limit_bytes=56 * MIB),
        name="ocean",
    )(src, count, sw, sh, blocks, weights, kernel_ocean, w_in, w_out, w_couple)


def body(
    atmosphere, ocean, kernel_atm, w_in_atm, w_out_atm, w_flux, kernel_ocean, w_in_ocean,
    w_out_ocean, w_couple, intersection_src, intersection_count, intersection_weight,
):
    aw, ah, sw, sh = exchange(atmosphere, ocean)
    atm_next, lat = atm_step(aw, ah, kernel_atm.T, w_in_atm, w_out_atm, w_flux)
    blocks = gather(lat)
    ocean_next = ocean_step(
        intersection_src[0].T, intersection_count[0], sw, sh, blocks, intersection_weight[0],
        kernel_ocean.T, w_in_ocean, w_out_ocean, w_couple.T,
    )
    return (atm_next, ocean_next)


def solution(mesh):
    return jax.shard_map(
        body,
        mesh=mesh,
        in_specs=(
            P(None, "face", "tile"),
            P(None, "tile", "face"),
            P(), P(), P(), P(), P(), P(), P(), P(),
            P("face", "tile", None),
            P("face", "tile"),
            P("face", "tile", None, None, None),
        ),
        out_specs=(P(None, "face", "tile"), P(None, "tile", "face")),
        check_vma=False,
    )
```

time: 328 us -> 194 us (0.59)
  Pallas kernels: 0 us -> 187 us
  other arithmetic: 132 us -> 0 us
  matrix products: 68.7 us -> 0 us
  waiting for transfers between devices: 46.1 us -> 0 us
  local copies, waits for them, and re-layouts: 38 us -> 2.41 us
  starting transfers between devices: 23.7 us -> 0 us
  between operations: 14.7 us -> 0.67 us
    pallas_call x0 -> x4, Pallas kernels: none -> 187 us  [the longest x1 57.5 us: gather(): pl.pallas_call(gather_kernel, out_shape=jax.ShapeDtypeStruct((N_TILE, 16,...]
    reduce_sum x4 -> x0, other arithmetic: 119 us -> none  [the longest x2 115 us: normalize(): average = jnp.mean(values, axis=0, keepdims=True)]
    dot_general x7 -> x0, matrix products: 68.7 us -> none  [the longest x2 43.4 us: mixer(): return jnp.einsum('ch,hxy->cxy', w_out, hidden, precision=HIGHEST)]
    ppermute x11 -> x0, waiting for transfers between devices: 46.1 us -> none  [the longest x4 18.8 us: padded_2(): after = lax.ppermute(initial, axis, down)]
    ppermute x11 -> x0, starting transfers between devices: 23.6 us -> none  [the longest x4 10.9 us: padded_2(): before = lax.ppermute(last, axis, up)]
    unnamed x52 -> x12, local copies, waits for them, and re-layouts: 15.9 us -> 2.41 us
    concatenate x3 -> x0, other arithmetic: 11.8 us -> none  [padded_2(): array = jnp.concatenate([before, array, after], axis=dim)]
    ppermute x7 -> x0, local copies, waits for them, and re-layouts: 7.62 us -> none  [the longest x3 4.57 us: padded_2(): before = lax.ppermute(last, axis, up)]
  transfers between devices with their start and end apart: 12 -> 0, of which waited for: 8 -> 0; matrix products, arithmetic and copies ran while one was open for 19% -> 0% of each run, Pallas kernels for 0% -> 0%
where the time goes in v1:
time: 194 us; the launch traced here: 190 us
  Pallas kernels  187 us (96%)
  local copies, waits for them, and re-layouts  2.41 us (1%)
    pallas_call x1, Pallas kernels, gather(): pl.pallas_call(gather_kernel, out_shape=jax.ShapeDtypeStruct((N_TILE, 16,...  57.5 us
    pallas_call x1, Pallas kernels, exchange(): pl.pallas_call(halo_kernel, out_shape=(jax.ShapeDtypeStruct((AR + 6, CA,...  47.8 us
    pallas_call x1, Pallas kernels, ocean_step(): pl.pallas_call(ocean_kernel, grid=(OR // 2,), out_shape=jax.ShapeDtypeStr...  42.9 us
    pallas_call x1, Pallas kernels, atm_step(): pl.pallas_call(atm_kernel, out_shape=(jax.ShapeDtypeStruct((CA, AR, COLS)...  38.6 us

profile of v1, /device:TPU:1, one launch (start us, length us, event | category | flops | bytes accessed | tf_op | source)
XLA Modules:
  0.0 190.0 jit_solution(12567917596681139689)
XLA Ops:
  0.6 0.0 copy-start
  0.6 1.4 copy-done
  2.0 0.0 copy-start.2
  2.0 0.0 copy-start.3
  2.0 0.0 copy-start.4
  2.0 0.0 copy-start.5
  2.1 47.8 %halo.1 = (f32[14,192,256]{2,1,0:T(8,128)}, f32[14,192,128]{2,1,0:T(8,128)S(1)}, f32[22,96,256]{2,1,0:T(8,128)}, f32[22,96,128]{2,1,0:T(8,128)S(1)}) custom-call(f32[192,8,256]{2,1,0:T(8,128)S(1)} %copy-done, f32[96,16,256]{2,1,0:T(8,128)} %sea_hbm.1), custom_call_target="tpu_custom_call" | custom-call | tf_op jit(solution)/shard_map/halo/pallas_call | solution.py:274
  49.9 0.0 copy-start.1
  49.9 1.0 copy-done.1
  50.9 0.0 copy-done.2
  50.9 0.0 copy-done.3
  50.9 0.0 copy-done.4
  50.9 0.0 copy-done.5
  50.9 38.6 %atmosphere.1 = (f32[192,8,256]{2,1,0:T(8,128)}, f32[16,64,128]{2,1,0:T(8,128)S(1)}) custom-call(f32[14,192,256]{2,1,0:T(8,128)} %get-tuple-element.8.aw, f32[14,192,128]{2,1,0:T(8,128)S(1)} %get-tuple-element.9.ah, f32[49,192]{1,0:T(8,128)S(1)} %bitcast.8, f32[192,768]{1,0:T(8,128)S(1)} %copy-done.2, f32[192,768]{1,0:T(8,128)S(1)} %copy-done.3, ...), custom_call_target="tpu_custom_call" | custom-call | tf_op jit(solution)/shard_map/atmosphere/pallas_call | solution.py:338
  89.5 57.5 %gather.1.blocks = f32[16,16,64,128]{3,2,1,0:T(8,128)} custom-call(f32[16,64,128]{2,1,0:T(8,128)S(1)} %get-tuple-element.13.lat), custom_call_target="tpu_custom_call" | custom-call | tf_op jit(solution)/shard_map/gather/pallas_call | solution.py:418
  147.0 42.9 %ocean.1 = f32[96,16,256]{2,1,0:T(8,128)} custom-call(s32[4,32]{1,0:T(4,128)} %bitcast.12, s32[32]{0:T(128)} %bitcast.13, f32[22,96,256]{2,1,0:T(8,128)} %get-tuple-element.11.sw, f32[22,96,128]{2,1,0:T(8,128)} %copy-done.1, f32[16,16,64,128]{3,2,1,0:T(8,128)} %gather.1.blocks, f32[32,4,128,128]{3,2,1,0:T(8,128)} %bitcast.9, f32[49,96]{1,0:T(8,128)} %bitcast.11, ...), custom_call_target="tpu_custom_call" | custom-call | tf_op jit(solution)/shard_map/ocean/pallas_call | solution.py:483
Async XLA Ops:
  0.6 1.4 copy-start
  2.0 48.9 %copy-start.2 = (f32[192,768]{1,0:T(8,128)S(1)}, f32[192,768]{1,0:T(8,128)}, u32[]{:S(2)}) copy-start(f32[192,768]{1,0:T(8,128)} %w_in_ref.2) | copy-start | bytes 1769476
  2.0 48.9 %copy-start.3 = (f32[192,768]{1,0:T(8,128)S(1)}, f32[192,768]{1,0:T(8,128)}, u32[]{:S(2)}) copy-start(f32[192,768]{1,0:T(8,128)} %w_out_ref.2) | copy-start | bytes 1769476
  2.0 48.9 %copy-start.4 = (f32[64,192]{1,0:T(8,128)S(1)}, f32[64,192]{1,0:T(8,128)}, u32[]{:S(2)}) copy-start(f32[64,192]{1,0:T(8,128)} %w_flux_ref.1) | copy-start | bytes 147460
  2.0 48.9 %copy-start.5 = (f32[192,49]{0,1:T(8,128)S(1)}, f32[192,49]{0,1:T(8,128)}, u32[]{:S(2)}) copy-start(f32[192,49]{0,1:T(8,128)} %param.15) | copy-start | bytes 112900
  49.9 1.0 copy-start.1

commit v2 on v0

v2 whole, which is shorter than its diff:
```python
import jax
import jax.numpy as jnp
from jax import lax
from jax.experimental import pallas as pl
from jax.experimental.pallas import tpu as pltpu
from jax.sharding import PartitionSpec as P

F32 = jnp.float32
BF16 = jnp.bfloat16
MESH = pl.DeviceIdType.MESH
MIB = 2**20
VMEM = pl.BlockSpec(memory_space=pltpu.VMEM)
SMEM = pl.BlockSpec(memory_space=pltpu.SMEM)
ANY = pl.BlockSpec(memory_space=pl.ANY)
DMA = pltpu.SemaphoreType.DMA

CA, HA, CO, HO, FL = 192, 768, 96, 384, 64
AR, OR, COLS = 8, 16, 256
N_FACE, N_TILE = 8, 16
EDGE = 8
STAGES = ((3, 4), (2, 5), (1, 6), (0, 7))
PIECES = ((3, 4, 5, 6, 7), (8, 9, 10, 11, 12), (0, 1, 2), (13, 14, 15))


def split(x):
    hi = x.astype(BF16)
    return hi, (x - hi.astype(F32)).astype(BF16)


def mm(a, b):
    return jnp.dot(a, b, preferred_element_type=F32)


def mm_t(a, b):
    return lax.dot_general(a, b, (((1,), (1,)), ((), ())), preferred_element_type=F32)


def gelu(x):
    return 0.5 * x * (1.0 + lax.erf(x * 0.7071067811865476))


def lane_sum(x, ones):
    hi, rest = x.astype(BF16), x
    rest = rest - hi.astype(F32)
    mid, low = split(rest)
    return mm(hi, ones) + (mm(mid, ones) + mm(low, ones))


def one_where(condition):
    return jnp.where(condition, 1.0, 0.0).astype(BF16)


def swap_halves(x):
    return pltpu.roll(x, 64, 1)


def rows_out_of(raw, rows, channels, wide):
    for half in range(2):
        flat = raw.at[half].reshape(channels * rows, 128)
        for r in range(rows):
            wide[r, :, half * 128 : half * 128 + 128] = flat[pl.ds(r, channels, stride=rows), :]


def turn_atm(wide, turned_a, turned_b, row):
    for half in range(2):
        cut = slice(half * 128, half * 128 + 128)
        turned_a[row, EDGE + half * 128 : EDGE + half * 128 + 128, :] = jnp.transpose(wide[row, 0:128, cut])
    both = jnp.concatenate([wide[row, 128:CA, 0:128], wide[row, 128:CA, 128:256]], axis=0)
    turned_b[row, EDGE : EDGE + 128, :] = jnp.transpose(both)


def turn_sea(values, turned, row):
    for half in range(2):
        cut = slice(half * 128, half * 128 + 128)
        full = jnp.concatenate([values[:, cut], jnp.zeros((128 - CO, 128), F32)], axis=0)
        turned[row, EDGE + half * 128 : EDGE + half * 128 + 128, :] = jnp.transpose(full)


def depthwise(src, taps, tops, cols, out, m):
    needed = sorted({t + i for t in tops for i in range(7)})

    def step(g, carry):
        start = g * (8 * m)
        sums = [[jnp.zeros((8, 128), F32) for _ in range(m)] for _ in tops]
        for j in range(7):
            weights = [taps[i * 7 + j] for i in range(7)]
            for row in needed:
                for b in range(m):
                    v = src[row, pl.ds(start + (8 * b + EDGE - 3 + j), 8), :]
                    for n, t in enumerate(tops):
                        if 0 <= row - t < 7:
                            sums[n][b] = sums[n][b] + weights[row - t] * v
        for n in range(len(tops)):
            for b in range(m):
                out[n, pl.ds(pl.multiple_of(start + 8 * b, 8), 8), :] = sums[n][b]
        return carry

    lax.fori_loop(0, cols // (8 * m), step, 0)


def ring(value, step, count):
    return lax.rem(value + (step + count), count)


def fused_kernel(
    src, count, atm_hbm, sea_hbm, weights_hbm,
    kernel_atm, w_in_atm, w_out_atm, w_flux, kernel_sea, w_in_sea, w_out_sea, w_couple,
    atm_out, sea_out,
    atm_raw, sea_raw, aw, ata, atb, sw, st,
    a_out, a_in, s_out, s_in, mirror_w, mirror_out, mirror_in,
    taps_a, taps_b, taps_s, conv_a, conv_b, conv_s,
    wi_a, wo_a, wf_a, hidden, wi_s, wo_s, wic_s, pre, blocks, slots, w_hi, w_lo, back_a, back_s,
    load_sem, slot_sem, out_sem, send_sem, recv_sem, flux_send, flux_recv,
):
    face, tile = lax.axis_index("face"), lax.axis_index("tile")
    up, down = ring(face, 1, N_FACE), ring(face, -1, N_FACE)
    north, south = ring(tile, 1, N_TILE), ring(tile, -1, N_TILE)
    y, x, core = tile // 4, lax.rem(tile // 2, 2), lax.rem(tile, 2)
    top = tile == N_TILE - 1
    across = (N_FACE - 1 - face, tile)

    def at(dy, dx, dc):
        return (ring(y, dy, 4) * 2 + lax.rem(x + dx, 2)) * 2 + lax.rem(core + dc, 2)

    partner, sibling = at(0, 1, 0), at(0, 0, 1)

    loads = []
    for half in range(2):
        cut = pl.ds(128 * half, 128)
        loads.append(pltpu.make_async_copy(atm_hbm.at[:, :, cut], atm_raw.at[half], load_sem.at[half]))
    for half in range(2):
        cut = pl.ds(128 * half, 128)
        loads.append(pltpu.make_async_copy(sea_hbm.at[:, :, cut], sea_raw.at[half], load_sem.at[2 + half]))
    for load in loads:
        load.start()

    def weight_load(n):
        return pltpu.make_async_copy(weights_hbm.at[pl.ds(4 * n, 4)], slots.at[n % 2], slot_sem.at[n % 2])

    weight_load(0).start()
    weight_load(1).start()

    barrier = pltpu.get_barrier_semaphore()
    near = [
        (up, tile), (down, tile), (face, north), (face, south),
        (up, north), (up, south), (down, north), (down, south),
        (face, partner), (face, at(1, 0, 0)), (face, at(-1, 0, 0)), (face, at(2, 0, 0)),
    ]
    for device in near:
        pl.semaphore_signal(barrier, inc=1, device_id=device, device_id_type=MESH)

    @pl.when(top)
    def _():
        pl.semaphore_signal(barrier, inc=1, device_id=across, device_id_type=MESH)

    def copy(k, src_ref, dst_ref, device):
        return pltpu.make_async_remote_copy(
            src_ref=src_ref, dst_ref=dst_ref, send_sem=send_sem.at[k], recv_sem=recv_sem.at[k],
            device_id=device, device_id_type=MESH,
        )

    loads[0].wait()
    loads[1].wait()
    rows_out_of(atm_raw, AR, CA, aw.at[pl.ds(3, AR)])
    pl.semaphore_wait(barrier, len(near) + tile // (N_TILE - 1))
    row_copies = []
    for d in range(3):
        row_copies.append(copy(2 * d, aw.at[10 - d], aw.at[2 - d], (up, tile)))
        row_copies.append(copy(2 * d + 1, aw.at[3 + d], aw.at[11 + d], (down, tile)))
    for c in row_copies:
        c.start()

    for r in range(AR):
        turn_atm(aw, ata, atb, 3 + r)
    for r in range(AR):
        to = pl.ds(4 * r, 3)
        a_out[0, to, :] = ata[3 + r, pl.ds(EDGE + COLS - 3, 3), :]
        a_out[1, to, :] = ata[3 + r, pl.ds(EDGE, 3), :]
        to = pl.ds(32 + 4 * r, 3)
        a_out[0, to, :] = swap_halves(atb[3 + r, pl.ds(EDGE + 125, 3), :])
        a_out[1, to, :] = swap_halves(atb[3 + r, pl.ds(EDGE, 3), :])
    edge_copies = []
    for n, f in enumerate((up, face, down)):
        edge_copies.append(copy(6 + n, a_out.at[0], a_in.at[0, n], (f, north)))
        edge_copies.append(copy(9 + n, a_out.at[1], a_in.at[1, n], (f, south)))
    for n in (2, 3, 0, 1, 4, 5):
        edge_copies[n].start()

    def atm_edges(row):
        n = 0 if row < 3 else 1 if row < 3 + AR else 2
        r = (row - 3) % AR
        low = lax.broadcasted_iota(jnp.int32, (3, 128), 1) < 64
        frm = pl.ds(4 * r, 3)
        ata[row, pl.ds(EDGE - 3, 3), :] = a_in[0, n, frm, :]
        ata[row, pl.ds(EDGE + COLS, 3), :] = a_in[1, n, frm, :]
        frm = pl.ds(32 + 4 * r, 3)
        inner = swap_halves(atb[row, pl.ds(EDGE + 125, 3), :])
        outer = swap_halves(atb[row, pl.ds(EDGE, 3), :])
        atb[row, pl.ds(EDGE - 3, 3), :] = jnp.where(low, a_in[0, n, frm, :], inner)
        atb[row, pl.ds(EDGE + 128, 3), :] = jnp.where(low, outer, a_in[1, n, frm, :])

    for t in range(49):
        k = kernel_atm[t : t + 1, :]
        taps_a[t] = jnp.broadcast_to(k[:, 0:128], (8, 128))
        taps_b[t] = jnp.broadcast_to(jnp.concatenate([k[:, 128:CA], k[:, 128:CA]], axis=1), (8, 128))
    turned = jnp.transpose(w_in_atm[...])
    gap = jnp.zeros((HA, 64), F32)
    for n, full in enumerate(
        (jnp.concatenate([turned, gap], axis=1), jnp.concatenate([turned[:, 0:128], gap, turned[:, 128:CA]], axis=1))
    ):
        hi, lo = split(full)
        for c in range(3):
            wi_a[n, c, 0:256, :] = hi[256 * c : 256 * c + 256]
            wi_a[n, c, 256:512, :] = lo[256 * c : 256 * c + 256]
    wo_a[0:CA, :], wo_a[CA : 2 * CA, :] = split(w_out_atm[...])
    wf_a[0:FL, :], wf_a[FL : 2 * FL, :] = split(w_flux[...])
    depth = lax.broadcasted_iota(jnp.int32, (256, 128), 0)
    lane = lax.broadcasted_iota(jnp.int32, (256, 128), 1)
    ones_first = one_where(depth < CA)
    ones_second = one_where((depth < 128) | (depth >= CA))

    def mm_stacked(stack, size, right):
        both = mm(stack, right[0])
        return both[0:size] + (both[size : 2 * size] + mm(stack[0:size], right[1]))

    def atm_stage(stage):
        tops = STAGES[stage]
        depthwise(ata, taps_a, tops, 256, conv_a, 4)
        depthwise(atb, taps_b, tops, 128, conv_b, 4)
        b = jnp.concatenate([conv_b[0], conv_b[1]], axis=0)
        a1 = jnp.concatenate([conv_a[0, 0:128], conv_a[1, 0:128]], axis=0)
        a2 = jnp.concatenate([conv_a[0, 128:256], conv_a[1, 128:256]], axis=0)
        m1 = lane_sum(jnp.concatenate([a1, b], axis=1), ones_first) * (1.0 / CA)
        m2 = lane_sum(jnp.concatenate([a2, b], axis=1), ones_second) * (1.0 / CA)
        a1, a2, b = a1 - m1, a2 - m2, b - jnp.where(lane < 64, m1, m2)
        v1 = lane_sum(jnp.concatenate([a1 * a1, b * b], axis=1), ones_first) * (1.0 / CA)
        v2 = lane_sum(jnp.concatenate([a2 * a2, b * b], axis=1), ones_second) * (1.0 / CA)
        r1, r2 = lax.rsqrt(v1 + 1e-06), lax.rsqrt(v2 + 1e-06)
        b = b * jnp.where(lane < 64, r1, r2)
        normed = (
            split(jnp.concatenate([a1 * r1, b], axis=1)),
            split(jnp.concatenate([a2 * r2, b], axis=1)),
        )
        for c in range(3):
            for half in range(2):
                hi, lo = normed[half]
                both = mm_t(wi_a[half, c], hi)
                value = gelu(both[0:256] + (both[256:512] + mm_t(wi_a[half, c, 0:256], lo)))
                to = (slice(256 * c, 256 * c + 256), slice(256 * half, 256 * half + 256))
                hidden[(0, *to)], hidden[(1, *to)] = split(value)
        for half in range(2):
            cut = slice(256 * half, 256 * half + 256)
            mixed = mm_stacked(wo_a[...], CA, (hidden[0, :, cut], hidden[1, :, cut]))
            here = slice(half * 128, half * 128 + 128)
            value = mixed + jnp.concatenate([aw[3 + row, :, here] for row in tops], axis=1)
            flux = mm_stacked(wf_a[...], FL, split(value))
            for n, row in enumerate(tops):
                part = slice(n * 128, n * 128 + 128)
                blocks[tile, 4 * stage + 2 * n + half] = flux[:, part]
                back_a.at[half].reshape(CA * AR, 128)[pl.ds(row, CA, stride=AR), :] = value[:, part]

    def flux_copy(stage, kind, block, target):
        part = blocks.at[block, pl.ds(4 * stage, 4)]
        return pltpu.make_async_remote_copy(
            src_ref=part, dst_ref=part, send_sem=flux_send.at[stage, kind], recv_sem=flux_recv.at[stage, kind],
            device_id=(face, target), device_id_type=MESH,
        )

    hops = ((1, 1), (2, -1), (3, 2))
    sent = []

    def start(mine):
        for c in mine:
            c.start()
        sent.extend(mine)

    def send_own(stage):
        start([flux_copy(stage, 0, tile, partner)])
        start([flux_copy(stage, kind, tile, at(dy, 0, 0)) for kind, dy in hops])
        start([flux_copy(stage, 7, tile, sibling)])

    def relay(stage):
        flux_copy(stage, 0, partner, partner).wait_recv()
        start([flux_copy(stage, kind + 3, partner, at(dy, 0, 0)) for kind, dy in hops])
        start([flux_copy(stage, 8, partner, sibling)])

    def forward(stage, hop):
        for kind, dy in hops:
            block = at(-dy, hop, 0)
            flux_copy(stage, kind + 3 * hop, block, partner).wait_recv()
            start([flux_copy(stage, 8 + kind + 3 * hop, block, sibling)])

    def finish(stage):
        flux_copy(stage, 7, sibling, partner).wait_recv()
        flux_copy(stage, 8, at(0, 1, 1), partner).wait_recv()
        for hop in range(2):
            for kind, dy in hops:
                flux_copy(stage, 8 + kind + 3 * hop, at(-dy, hop, 1), partner).wait_recv()

    for n in (2, 3):
        edge_copies[n].wait_recv()
    for r in range(AR):
        atm_edges(3 + r)
    atm_stage(0)
    send_own(0)

    loads[2].wait()
    loads[3].wait()
    rows_out_of(sea_raw, OR, CO, sw.at[pl.ds(3, OR)])
    sea_copies = [
        copy(12, sw.at[pl.ds(16, 3)], sw.at[pl.ds(0, 3)], (face, north)),
        copy(13, sw.at[pl.ds(3, 3)], sw.at[pl.ds(19, 3)], (face, south)),
    ]
    for r in range(OR):
        turn_sea(sw[3 + r], st, 3 + r)
    for r in range(OR):
        to = pl.ds(4 * r, 3)
        s_out[0, to, :] = st[3 + r, pl.ds(EDGE + COLS - 3, 3), :]
        s_out[1, to, :] = st[3 + r, pl.ds(EDGE, 3), :]
    for n, t in enumerate((north, tile, south)):
        sea_copies.append(copy(14 + n, s_out.at[0], s_in.at[0, n], (up, t)))
        sea_copies.append(copy(17 + n, s_out.at[1], s_in.at[1, n], (down, t)))
    for c in sea_copies[2:]:
        c.start()
    for t in range(49):
        k = jnp.concatenate([kernel_sea[t : t + 1, :], jnp.zeros((1, 128 - CO), F32)], axis=1)
        taps_s[t] = jnp.broadcast_to(k, (8, 128))
    turned = jnp.transpose(w_in_sea[...])
    hi, lo = split(jnp.concatenate([turned, jnp.zeros((HO, 128 - CO), F32)], axis=1))
    wi_s[:, 0:128] = hi
    wi_s[:, 128:256] = lo
    wo_s[0:CO, :], wo_s[CO : 2 * CO, :] = split(w_out_sea[...])
    left = split(turned)
    right = split(jnp.transpose(w_couple[...]))
    hi, lo = split(mm(left[0], right[0]) + (mm(left[1], right[0]) + mm(left[0], right[1])))
    wic_s[...] = jnp.concatenate([hi, hi, lo], axis=1)
    ones_sea = one_where(depth[0:128] < CO)

    def sea_edges(row, n, r):
        frm = pl.ds(4 * r, 3)
        st[row, pl.ds(EDGE - 3, 3), :] = s_in[0, n, frm, :]
        st[row, pl.ds(EDGE + COLS, 3), :] = s_in[1, n, frm, :]

    def sea_piece(piece):
        tops = PIECES[piece]
        depthwise(st, taps_s, tops, 256, conv_s, 2)
        for n, row in enumerate(tops):
            c = conv_s[n]
            c = c - lane_sum(c, ones_sea) * (1.0 / CO)
            spread = lane_sum(c * c, ones_sea) * (1.0 / CO)
            hi, lo = split(c * lax.rsqrt(spread + 1e-06))
            pre[row] = mm_t(wi_s[...], jnp.concatenate([hi, hi], axis=1)) + mm_t(wi_s[:, 0:128], lo)

    def split_weights(n):
        weight_load(n).wait()

        def step(b, carry):
            w_hi[4 * n + b], w_lo[4 * n + b] = split(slots[n % 2, b].reshape(512, 128))
            return carry

        lax.fori_loop(0, 4, step, 0)
        if n + 2 < 8:
            weight_load(n + 2).start()

    for n in (2, 3):
        sea_copies[2 + n].wait_recv()
    for r in range(OR):
        sea_edges(3 + r, 1, r)
    sea_piece(0)

    def atm_rows(d):
        row_copies[2 * d].wait_recv()
        row_copies[2 * d + 1].wait_recv()
        if d == 0:
            for n in (0, 1, 4, 5):
                edge_copies[n].wait_recv()
        for row in (2 - d, 11 + d):
            turn_atm(aw, ata, atb, row)
            atm_edges(row)

    atm_rows(0)
    atm_stage(1)
    send_own(1)
    relay(0)
    for c in sea_copies[:2]:
        c.start()

    fold = [
        copy(20, sw.at[pl.ds(16, 3)], mirror_w, across),
        copy(21, mirror_out, mirror_in, across),
    ]

    @pl.when(top)
    def _():
        for r in range(3):
            mirror_out[pl.ds(8 * r, 3), :] = st[16 + r, pl.ds(EDGE - 3, 3), :]
            mirror_out[pl.ds(8 * r + 4, 3), :] = st[16 + r, pl.ds(EDGE + COLS, 3), :]
        for c in fold:
            c.start()

    sea_piece(1)
    split_weights(0)
    split_weights(1)
    atm_rows(1)
    atm_stage(2)
    send_own(2)
    relay(1)
    forward(0, 0)
    split_weights(2)
    split_weights(3)
    atm_rows(2)
    atm_stage(3)
    send_own(3)
    relay(2)
    forward(0, 1)
    forward(1, 0)
    atm_store = []
    for half in range(2):
        cut = pl.ds(128 * half, 128)
        atm_store.append(pltpu.make_async_copy(back_a.at[half], atm_out.at[:, :, cut], out_sem.at[half]))
    for c in atm_store:
        c.start()
    for n in range(4, 8):
        split_weights(n)
    relay(3)
    forward(1, 1)
    forward(2, 0)

    for n in (0, 1, 4, 5):
        sea_copies[2 + n].wait_recv()
    for c in sea_copies[:2]:
        c.wait_recv()
    for r in range(3):
        turn_sea(sw[r], st, r)
        sea_edges(r, 0, OR - 3 + r)
        turn_sea(sw[3 + OR + r], st, 3 + OR + r)
        sea_edges(3 + OR + r, 2, r)

    @pl.when(tile == 0)
    def _():
        st[0:3] = jnp.zeros((3, COLS + 2 * EDGE, 128), F32)

    @pl.when(top)
    def _():
        for c in fold:
            c.wait()
        flip = 127 - lax.broadcasted_iota(jnp.int32, (CO, 128), 1)
        for k in range(3):
            first = jnp.take_along_axis(mirror_w[2 - k, :, 128:256], flip, axis=1)
            second = jnp.take_along_axis(mirror_w[2 - k, :, 0:128], flip, axis=1)
            turn_sea(jnp.concatenate([first, second], axis=1), st, 19 + k)
            for c in range(3):
                st[19 + k, pl.ds(EDGE - 3 + c, 1), :] = mirror_in[pl.ds(8 * (2 - k) + 4 + 2 - c, 1), :]
                st[19 + k, pl.ds(EDGE + COLS + c, 1), :] = mirror_in[pl.ds(8 * (2 - k) + 2 - c, 1), :]

    sea_piece(2)
    sea_piece(3)
    forward(2, 1)
    forward(3, 0)
    forward(3, 1)
    for stage in range(4):
        finish(stage)

    def sea_row(q):
        fluxes = []
        for half in range(2):
            block = 2 * q + half
            live = count[block]
            picked = []
            for k in range(4):
                index = src[k, block]
                t, a = index // 16, lax.rem(index, 16)
                r = a // 2
                spot = jnp.where(r < 4, (3 - r) * 4, (r - 4) * 4 + 2) + lax.rem(a, 2)
                picked.append(jnp.where(k < live, blocks[t, spot], 0.0))
            hi, lo = split(jnp.concatenate(picked, axis=1))
            both = mm(jnp.concatenate([hi, lo], axis=0), w_hi[block])
            fluxes.append(both[0:FL] + (both[FL : 2 * FL] + mm(hi, w_lo[block])))
        hi, lo = split(jnp.concatenate(fluxes, axis=1))
        grown = split(gelu(pre[q] + mm(wic_s[...], jnp.concatenate([hi, lo, hi], axis=0))))
        value = sw[3 + q] + mm_stacked(wo_s[...], CO, grown)
        for half in range(2):
            flat = back_s.at[half].reshape(CO * OR, 128)
            flat[pl.ds(q, CO, stride=OR), :] = value[:, half * 128 : half * 128 + 128]

    sea_store = []
    for part in range(2):

        def step(i, carry, part=part):
            sea_row(8 * part + 2 * i)
            sea_row(8 * part + 2 * i + 1)
            return carry

        lax.fori_loop(0, 4, step, 0)
        for half in range(2):
            rows, cut = pl.ds(8 * part, 8), pl.ds(128 * half, 128)
            c = pltpu.make_async_copy(
                back_s.at[half, :, rows], sea_out.at[:, rows, cut], out_sem.at[2 + 2 * part + half]
            )
            c.start()
            sea_store.append(c)
    for c in row_copies + edge_copies + sea_copies + sent:
        c.wait_send()
    for c in atm_store + sea_store:
        c.wait()


def step(src, count, atmosphere, ocean, weights, *params):
    return pl.pallas_call(
        fused_kernel,
        out_shape=(
            jax.ShapeDtypeStruct((CA, AR, COLS), F32),
            jax.ShapeDtypeStruct((CO, OR, COLS), F32),
        ),
        in_specs=[SMEM, SMEM, ANY, ANY, ANY] + [VMEM] * 8,
        out_specs=(ANY, ANY),
        scratch_shapes=[
            pltpu.VMEM((2, CA, AR, 128), F32),
            pltpu.VMEM((2, CO, OR, 128), F32),
            pltpu.VMEM((AR + 6, CA, COLS), F32),
            pltpu.VMEM((AR + 6, COLS + 2 * EDGE, 128), F32),
            pltpu.VMEM((AR + 6, 128 + 2 * EDGE, 128), F32),
            pltpu.VMEM((OR + 6, CO, COLS), F32),
            pltpu.VMEM((OR + 6, COLS + 2 * EDGE, 128), F32),
            pltpu.VMEM((2, 64, 128), F32),
            pltpu.VMEM((2, 3, 64, 128), F32),
            pltpu.VMEM((2, 64, 128), F32),
            pltpu.VMEM((2, 3, 64, 128), F32),
            pltpu.VMEM((3, CO, COLS), F32),
            pltpu.VMEM((24, 128), F32),
            pltpu.VMEM((24, 128), F32),
            pltpu.VMEM((49, 8, 128), F32),
            pltpu.VMEM((49, 8, 128), F32),
            pltpu.VMEM((49, 8, 128), F32),
            pltpu.VMEM((2, 256, 128), F32),
            pltpu.VMEM((2, 128, 128), F32),
            pltpu.VMEM((5, 256, 128), F32),
            pltpu.VMEM((2, 3, 512, 256), BF16),
            pltpu.VMEM((2 * CA, HA), BF16),
            pltpu.VMEM((2 * FL, CA), BF16),
            pltpu.VMEM((2, HA, 2 * COLS), BF16),
            pltpu.VMEM((HO, 256), BF16),
            pltpu.VMEM((2 * CO, HO), BF16),
            pltpu.VMEM((HO, 3 * FL), BF16),
            pltpu.VMEM((OR, HO, COLS), F32),
            pltpu.VMEM((N_TILE, 16, FL, 128), F32),
            pltpu.VMEM((2, 4, 4, 128, 128), F32),
            pltpu.VMEM((32, 512, 128), BF16),
            pltpu.VMEM((32, 512, 128), BF16),
            pltpu.VMEM((2, CA, AR, 128), F32),
            pltpu.VMEM((2, CO, OR, 128), F32),
            DMA((4,)),
            DMA((2,)),
            DMA((6,)),
            DMA((22,)),
            DMA((22,)),
            DMA((4, 15)),
            DMA((4, 15)),
        ],
        compiler_params=pltpu.CompilerParams(
            collective_id=0, has_side_effects=True, vmem_limit_bytes=58 * MIB
        ),
        name="coupled",
    )(src, count, atmosphere, ocean, weights, *params)


def body(
    atmosphere, ocean, kernel_atm, w_in_atm, w_out_atm, w_flux, kernel_ocean, w_in_ocean,
    w_out_ocean, w_couple, intersection_src, intersection_count, intersection_weight,
):
    return step(
        intersection_src[0].T, intersection_count[0], atmosphere, ocean, intersection_weight[0],
        kernel_atm.T, w_in_atm, w_out_atm, w_flux, kernel_ocean.T, w_in_ocean, w_out_ocean, w_couple.T,
    )


def solution(mesh):
    return jax.shard_map(
        body,
        mesh=mesh,
        in_specs=(
            P(None, "face", "tile"),
            P(None, "tile", "face"),
            P(), P(), P(), P(), P(), P(), P(), P(),
            P("face", "tile", None),
            P("face", "tile"),
            P("face", "tile", None, None, None),
        ),
        out_specs=(P(None, "face", "tile"), P(None, "tile", "face")),
        check_vma=False,
    )
```

time: 328 us -> 125 us (0.38); the launches traced: 324 us -> 125 us
  other arithmetic: 132 us -> 0 us
  Pallas kernels: 0 us -> 120 us
  matrix products: 68.7 us -> 0 us
  waiting for transfers between devices: 46.1 us -> 0 us
  local copies, waits for them, and re-layouts: 38 us -> 3.92 us
  starting transfers between devices: 23.7 us -> 0 us
  between operations: 14.7 us -> 0.65 us
    pallas_call x0 -> x1, Pallas kernels: none -> 120 us  [step(): pl.pallas_call(fused_kernel, out_shape=(jax.ShapeDtypeStruct((CA, AR, COL...]
    reduce_sum x4 -> x0, other arithmetic: 119 us -> none  [the longest x2 115 us: normalize(): average = jnp.mean(values, axis=0, keepdims=True)]
    dot_general x7 -> x0, matrix products: 68.7 us -> none  [the longest x2 43.4 us: mixer(): return jnp.einsum('ch,hxy->cxy', w_out, hidden, precision=HIGHEST)]
    ppermute x11 -> x0, waiting for transfers between devices: 46.1 us -> none  [the longest x4 18.8 us: padded_2(): after = lax.ppermute(initial, axis, down)]
    ppermute x11 -> x0, starting transfers between devices: 23.6 us -> none  [the longest x4 10.9 us: padded_2(): before = lax.ppermute(last, axis, up)]
    unnamed x52 -> x4, local copies, waits for them, and re-layouts: 15.9 us -> 3.92 us
    concatenate x3 -> x0, other arithmetic: 11.8 us -> none  [padded_2(): array = jnp.concatenate([before, array, after], axis=dim)]
    ppermute x7 -> x0, local copies, waits for them, and re-layouts: 7.62 us -> none  [the longest x3 4.57 us: padded_2(): before = lax.ppermute(last, axis, up)]
  transfers between devices with their start and end apart: 12 -> 0, of which waited for: 8 -> 0; matrix products, arithmetic and copies ran while one was open for 19% -> 0% of each run, Pallas kernels for 0% -> 0%
where the time goes in v2:
time: 125 us
  Pallas kernels  120 us (96%)
  local copies, waits for them, and re-layouts  3.92 us (3%)
    pallas_call x1, Pallas kernels, step(): pl.pallas_call(fused_kernel, out_shape=(jax.ShapeDtypeStruct((CA, AR, COL...  120 us
    unnamed x4, local copies, waits for them, and re-layouts  3.92 us

profile of v2, /device:TPU:1, one launch (start us, length us, event | category | flops | bytes accessed | tf_op | source)
XLA Modules:
  0.0 124.8 jit_solution(2024491560265178183)
XLA Ops:
  0.6 120.3 %coupled.1 = (f32[192,8,256]{2,1,0:T(8,128)}, f32[96,16,256]{2,1,0:T(8,128)}) custom-call(s32[4,32]{1,0:T(4,128)} %bitcast.12, s32[32]{0:T(128)} %bitcast.13, f32[192,8,256]{2,1,0:T(8,128)} %atm_hbm.1, f32[96,16,256]{2,1,0:T(8,128)} %sea_hbm.1, f32[32,4,128,128]{3,2,1,0:T(8,128)} %bitcast.8, f32[49,192]{1,0:T(8,128)} %bitcast.9, f32[192,768]{1,0:T(8,128)} %w_in_atm.1, ...), custom_call_target="tpu_custom_call" | custom-call | tf_op jit(solution)/shard_map/coupled/pallas_call | solution.py:509
  120.9 0.0 copy-start
  120.9 2.8 %copy.17 = f32[192,8,256]{2,1,0:T(8,128)} copy(f32[192,8,256]{2,1,0:T(8,128)} %get-tuple-element.4) | data formatting | bytes 3145728
  123.7 0.0 copy-done
  123.7 1.1 copy.18
Async XLA Ops:
  120.9 2.8 %copy-start = (f32[96,16,256]{2,1,0:T(8,128)S(1)}, f32[96,16,256]{2,1,0:T(8,128)}, u32[]{:S(2)}) copy-start(f32[96,16,256]{2,1,0:T(8,128)} %get-tuple-element.5) | copy-start | bytes 4718596

commit v3 on v2

--- a/solution.py
+++ b/solution.py
@@ -19,7 +19,7 @@
 N_FACE, N_TILE = 8, 16
 EDGE = 8
 STAGES = ((3, 4), (2, 5), (1, 6), (0, 7))
-PIECES = ((3, 4, 5, 6, 7), (8, 9, 10, 11, 12), (0, 1, 2), (13, 14, 15))
+PIECES = ((3, 8), (8, 13), (0, 3), (13, 16))
 
 
 def split(x):
@@ -39,11 +39,13 @@
     return 0.5 * x * (1.0 + lax.erf(x * 0.7071067811865476))
 
 
-def lane_sum(x, ones):
-    hi, rest = x.astype(BF16), x
-    rest = rest - hi.astype(F32)
-    mid, low = split(rest)
-    return mm(hi, ones) + (mm(mid, ones) + mm(low, ones))
+def lane_sum(x, ones, parts):
+    total = 0.0
+    for _ in range(parts):
+        part = x.astype(BF16)
+        x = x - part.astype(F32)
+        total = total + mm(part, ones)
+    return total
 
 
 def one_where(condition):
@@ -76,23 +78,23 @@
         turned[row, EDGE + half * 128 : EDGE + half * 128 + 128, :] = jnp.transpose(full)
 
 
-def depthwise(src, taps, tops, cols, out, m):
-    needed = sorted({t + i for t in tops for i in range(7)})
+def depthwise(src, taps, tops, rows, cols, out, m, add=False):
+    pairs = {row: [t for t in tops if 0 <= row - t < 7] for row in rows}
 
     def step(g, carry):
         start = g * (8 * m)
-        sums = [[jnp.zeros((8, 128), F32) for _ in range(m)] for _ in tops]
+        to = [pl.ds(pl.multiple_of(start + 8 * b, 8), 8) for b in range(m)]
+        sums = {t: [out[t, to[b], :] if add else jnp.zeros((8, 128), F32) for b in range(m)] for t in tops}
         for j in range(7):
-            weights = [taps[i * 7 + j] for i in range(7)]
-            for row in needed:
+            weights = {i: taps[i * 7 + j] for i in {row - t for row in rows for t in pairs[row]}}
+            for row in rows:
                 for b in range(m):
                     v = src[row, pl.ds(start + (8 * b + EDGE - 3 + j), 8), :]
-                    for n, t in enumerate(tops):
-                        if 0 <= row - t < 7:
-                            sums[n][b] = sums[n][b] + weights[row - t] * v
-        for n in range(len(tops)):
+                    for t in pairs[row]:
+                        sums[t][b] = sums[t][b] + weights[row - t] * v
+        for t in tops:
             for b in range(m):
-                out[n, pl.ds(pl.multiple_of(start + 8 * b, 8), 8), :] = sums[n][b]
+                out[t, to[b], :] = sums[t][b]
         return carry
 
     lax.fori_loop(0, cols // (8 * m), step, 0)
@@ -109,7 +111,7 @@
     atm_raw, sea_raw, aw, ata, atb, sw, st,
     a_out, a_in, s_out, s_in, mirror_w, mirror_out, mirror_in,
     taps_a, taps_b, taps_s, conv_a, conv_b, conv_s,
-    wi_a, wo_a, wf_a, hidden, wi_s, wo_s, wic_s, pre, blocks, slots, w_hi, w_lo, back_a, back_s,
+    wi_a, wo_a, wf_a, hidden, wi_s, wo_s, wic_s, pre, blocks, slots, w_cat, back_a, back_s,
     load_sem, slot_sem, out_sem, send_sem, recv_sem, flux_send, flux_recv,
 ):
     face, tile = lax.axis_index("face"), lax.axis_index("tile")
@@ -167,22 +169,23 @@
     for d in range(3):
         row_copies.append(copy(2 * d, aw.at[10 - d], aw.at[2 - d], (up, tile)))
         row_copies.append(copy(2 * d + 1, aw.at[3 + d], aw.at[11 + d], (down, tile)))
-    for c in row_copies:
+    for c in row_copies[0:2]:
         c.start()
 
     for r in range(AR):
         turn_atm(aw, ata, atb, 3 + r)
     for r in range(AR):
-        to = pl.ds(4 * r, 3)
+        to = pl.ds(16 * (r // 4) + 4 * r, 3)
         a_out[0, to, :] = ata[3 + r, pl.ds(EDGE + COLS - 3, 3), :]
         a_out[1, to, :] = ata[3 + r, pl.ds(EDGE, 3), :]
-        to = pl.ds(32 + 4 * r, 3)
+        to = pl.ds(16 * (r // 4) + 4 * r + 16, 3)
         a_out[0, to, :] = swap_halves(atb[3 + r, pl.ds(EDGE + 125, 3), :])
         a_out[1, to, :] = swap_halves(atb[3 + r, pl.ds(EDGE, 3), :])
     edge_copies = []
     for n, f in enumerate((up, face, down)):
-        edge_copies.append(copy(6 + n, a_out.at[0], a_in.at[0, n], (f, north)))
-        edge_copies.append(copy(9 + n, a_out.at[1], a_in.at[1, n], (f, south)))
+        part = (pl.ds(32, 32), pl.ds(0, 64), pl.ds(0, 32))[n]
+        edge_copies.append(copy(6 + n, a_out.at[0, part], a_in.at[0, n, part], (f, north)))
+        edge_copies.append(copy(9 + n, a_out.at[1, part], a_in.at[1, n, part], (f, south)))
     for n in (2, 3, 0, 1, 4, 5):
         edge_copies[n].start()
 
@@ -190,10 +193,10 @@
         n = 0 if row < 3 else 1 if row < 3 + AR else 2
         r = (row - 3) % AR
         low = lax.broadcasted_iota(jnp.int32, (3, 128), 1) < 64
-        frm = pl.ds(4 * r, 3)
+        frm = pl.ds(16 * (r // 4) + 4 * r, 3)
         ata[row, pl.ds(EDGE - 3, 3), :] = a_in[0, n, frm, :]
         ata[row, pl.ds(EDGE + COLS, 3), :] = a_in[1, n, frm, :]
-        frm = pl.ds(32 + 4 * r, 3)
+        frm = pl.ds(16 * (r // 4) + 4 * r + 16, 3)
         inner = swap_halves(atb[row, pl.ds(EDGE + 125, 3), :])
         outer = swap_halves(atb[row, pl.ds(EDGE, 3), :])
         atb[row, pl.ds(EDGE - 3, 3), :] = jnp.where(low, a_in[0, n, frm, :], inner)
@@ -223,18 +226,20 @@
         both = mm(stack, right[0])
         return both[0:size] + (both[size : 2 * size] + mm(stack[0:size], right[1]))
 
+    def atm_depthwise(tops, rows, m, add):
+        depthwise(ata, taps_a, tops, rows, 256, conv_a, m, add)
+        depthwise(atb, taps_b, tops, rows, 128, conv_b, m, add)
+
     def atm_stage(stage):
         tops = STAGES[stage]
-        depthwise(ata, taps_a, tops, 256, conv_a, 4)
-        depthwise(atb, taps_b, tops, 128, conv_b, 4)
-        b = jnp.concatenate([conv_b[0], conv_b[1]], axis=0)
-        a1 = jnp.concatenate([conv_a[0, 0:128], conv_a[1, 0:128]], axis=0)
-        a2 = jnp.concatenate([conv_a[0, 128:256], conv_a[1, 128:256]], axis=0)
-        m1 = lane_sum(jnp.concatenate([a1, b], axis=1), ones_first) * (1.0 / CA)
-        m2 = lane_sum(jnp.concatenate([a2, b], axis=1), ones_second) * (1.0 / CA)
+        b = jnp.concatenate([conv_b[t] for t in tops], axis=0)
+        a1 = jnp.concatenate([conv_a[t, 0:128] for t in tops], axis=0)
+        a2 = jnp.concatenate([conv_a[t, 128:256] for t in tops], axis=0)
+        m1 = lane_sum(jnp.concatenate([a1, b], axis=1), ones_first, 3) * (1.0 / CA)
+        m2 = lane_sum(jnp.concatenate([a2, b], axis=1), ones_second, 3) * (1.0 / CA)
         a1, a2, b = a1 - m1, a2 - m2, b - jnp.where(lane < 64, m1, m2)
-        v1 = lane_sum(jnp.concatenate([a1 * a1, b * b], axis=1), ones_first) * (1.0 / CA)
-        v2 = lane_sum(jnp.concatenate([a2 * a2, b * b], axis=1), ones_second) * (1.0 / CA)
+        v1 = lane_sum(jnp.concatenate([a1 * a1, b * b], axis=1), ones_first, 2) * (1.0 / CA)
+        v2 = lane_sum(jnp.concatenate([a2 * a2, b * b], axis=1), ones_second, 2) * (1.0 / CA)
         r1, r2 = lax.rsqrt(v1 + 1e-06), lax.rsqrt(v2 + 1e-06)
         b = b * jnp.where(lane < 64, r1, r2)
         normed = (
@@ -266,74 +271,118 @@
             device_id=(face, target), device_id_type=MESH,
         )
 
-    hops = ((1, 1), (2, -1), (3, 2))
     sent = []
 
-    def start(mine):
+    def start(*mine):
         for c in mine:
             c.start()
         sent.extend(mine)
 
+    def arrived(stage, kind, block):
+        flux_copy(stage, kind, block, partner).wait_recv()
+
     def send_own(stage):
-        start([flux_copy(stage, 0, tile, partner)])
-        start([flux_copy(stage, kind, tile, at(dy, 0, 0)) for kind, dy in hops])
-        start([flux_copy(stage, 7, tile, sibling)])
+        start(flux_copy(stage, 0, tile, partner))
+        start(flux_copy(stage, 1, tile, at(1, 0, 0)), flux_copy(stage, 2, tile, at(-1, 0, 0)))
+        if stage == 3:
+            start(flux_copy(stage, 3, tile, at(2, 0, 0)))
+        start(flux_copy(stage, 7, tile, sibling))
 
     def relay(stage):
-        flux_copy(stage, 0, partner, partner).wait_recv()
-        start([flux_copy(stage, kind + 3, partner, at(dy, 0, 0)) for kind, dy in hops])
-        start([flux_copy(stage, 8, partner, sibling)])
-
-    def forward(stage, hop):
-        for kind, dy in hops:
-            block = at(-dy, hop, 0)
-            flux_copy(stage, kind + 3 * hop, block, partner).wait_recv()
-            start([flux_copy(stage, 8 + kind + 3 * hop, block, sibling)])
+        arrived(stage, 0, partner)
+        start(flux_copy(stage, 4, partner, at(1, 0, 0)), flux_copy(stage, 5, partner, at(-1, 0, 0)))
+        if stage == 3:
+            start(flux_copy(stage, 6, partner, at(2, 0, 0)))
+        start(flux_copy(stage, 8, partner, sibling))
+
+    def near_own(stage):
+        arrived(stage, 1, at(-1, 0, 0))
+        if stage < 3:
+            start(flux_copy(stage, 3, at(-1, 0, 0), at(1, 0, 0)))
+        start(flux_copy(stage, 9, at(-1, 0, 0), sibling))
+        arrived(stage, 2, at(1, 0, 0))
+        start(flux_copy(stage, 10, at(1, 0, 0), sibling))
+
+    def near_relayed(stage):
+        arrived(stage, 5, at(1, 1, 0))
+        if stage < 3:
+            start(flux_copy(stage, 6, at(1, 1, 0), at(-1, 0, 0)))
+        start(flux_copy(stage, 13, at(1, 1, 0), sibling))
+        arrived(stage, 4, at(-1, 1, 0))
+        start(flux_copy(stage, 12, at(-1, 1, 0), sibling))
+
+    def far_own(stage):
+        arrived(stage, 3, at(2, 0, 0))
+        start(flux_copy(stage, 11, at(2, 0, 0), sibling))
+
+    def far_relayed(stage):
+        arrived(stage, 6, at(2, 1, 0))
+        start(flux_copy(stage, 14, at(2, 1, 0), sibling))
 
     def finish(stage):
-        flux_copy(stage, 7, sibling, partner).wait_recv()
-        flux_copy(stage, 8, at(0, 1, 1), partner).wait_recv()
+        arrived(stage, 7, sibling)
+        arrived(stage, 8, at(0, 1, 1))
         for hop in range(2):
-            for kind, dy in hops:
-                flux_copy(stage, 8 + kind + 3 * hop, at(-dy, hop, 1), partner).wait_recv()
+            arrived(stage, 9 + 3 * hop, at(-1, hop, 1))
+            arrived(stage, 10 + 3 * hop, at(1, hop, 1))
+            arrived(stage, 11 + 3 * hop, at(2, hop, 1))
+
+    def sea_start():
+        loads[2].wait()
+        loads[3].wait()
+        rows_out_of(sea_raw, OR, CO, sw.at[pl.ds(3, OR)])
+        sea_copies = [
+            copy(12, sw.at[pl.ds(16, 3)], sw.at[pl.ds(0, 3)], (face, north)),
+            copy(13, sw.at[pl.ds(3, 3)], sw.at[pl.ds(19, 3)], (face, south)),
+        ]
+        for r in range(OR):
+            turn_sea(sw[3 + r], st, 3 + r)
+        for r in range(OR):
+            to = pl.ds(4 * r, 3)
+            s_out[0, to, :] = st[3 + r, pl.ds(EDGE + COLS - 3, 3), :]
+            s_out[1, to, :] = st[3 + r, pl.ds(EDGE, 3), :]
+        for n, t in enumerate((north, tile, south)):
+            part = (pl.ds(48, 16), pl.ds(0, 64), pl.ds(0, 16))[n]
+            sea_copies.append(copy(14 + n, s_out.at[0, part], s_in.at[0, n, part], (up, t)))
+            sea_copies.append(copy(17 + n, s_out.at[1, part], s_in.at[1, n, part], (down, t)))
+        for c in sea_copies[2:]:
+            c.start()
+        return sea_copies
+
+    sea_copies = sea_start()
 
     for n in (2, 3):
         edge_copies[n].wait_recv()
     for r in range(AR):
         atm_edges(3 + r)
+    own = tuple(range(3, 3 + AR))
+    atm_depthwise((3, 4), own, 4, False)
     atm_stage(0)
     send_own(0)
-
-    loads[2].wait()
-    loads[3].wait()
-    rows_out_of(sea_raw, OR, CO, sw.at[pl.ds(3, OR)])
-    sea_copies = [
-        copy(12, sw.at[pl.ds(16, 3)], sw.at[pl.ds(0, 3)], (face, north)),
-        copy(13, sw.at[pl.ds(3, 3)], sw.at[pl.ds(19, 3)], (face, south)),
-    ]
-    for r in range(OR):
-        turn_sea(sw[3 + r], st, 3 + r)
-    for r in range(OR):
-        to = pl.ds(4 * r, 3)
-        s_out[0, to, :] = st[3 + r, pl.ds(EDGE + COLS - 3, 3), :]
-        s_out[1, to, :] = st[3 + r, pl.ds(EDGE, 3), :]
-    for n, t in enumerate((north, tile, south)):
-        sea_copies.append(copy(14 + n, s_out.at[0], s_in.at[0, n], (up, t)))
-        sea_copies.append(copy(17 + n, s_out.at[1], s_in.at[1, n], (down, t)))
-    for c in sea_copies[2:]:
+    for c in row_copies[2:4]:
         c.start()
-    for t in range(49):
-        k = jnp.concatenate([kernel_sea[t : t + 1, :], jnp.zeros((1, 128 - CO), F32)], axis=1)
-        taps_s[t] = jnp.broadcast_to(k, (8, 128))
-    turned = jnp.transpose(w_in_sea[...])
-    hi, lo = split(jnp.concatenate([turned, jnp.zeros((HO, 128 - CO), F32)], axis=1))
-    wi_s[:, 0:128] = hi
-    wi_s[:, 128:256] = lo
-    wo_s[0:CO, :], wo_s[CO : 2 * CO, :] = split(w_out_sea[...])
-    left = split(turned)
-    right = split(jnp.transpose(w_couple[...]))
-    hi, lo = split(mm(left[0], right[0]) + (mm(left[1], right[0]) + mm(left[0], right[1])))
-    wic_s[...] = jnp.concatenate([hi, hi, lo], axis=1)
+
+    def sea_parameters():
+        for t in range(49):
+            k = jnp.concatenate([kernel_sea[t : t + 1, :], jnp.zeros((1, 128 - CO), F32)], axis=1)
+            taps_s[t] = jnp.broadcast_to(k, (8, 128))
+        hi, lo = split(jnp.concatenate([w_in_sea[...], jnp.zeros((128 - CO, HO), F32)], axis=0))
+        wi_s[0:128] = hi
+        wi_s[128:256] = hi
+        wi_s[256:384] = lo
+        blank = jnp.zeros((HO, 128 - CO), F32)
+        hi, lo = split(jnp.concatenate([jnp.transpose(w_out_sea[...]), blank], axis=1))
+        wo_s[0:HO, 0:128] = hi
+        wo_s[0:HO, 128:256] = lo
+        wo_s[HO : 2 * HO, 0:128] = hi
+        wo_s[HO : 2 * HO, 128:256] = jnp.zeros((HO, 128), BF16)
+        left, right = split(w_couple[...]), split(w_in_sea[...])
+        hi, lo = split(mm(left[0], right[0]) + (mm(left[1], right[0]) + mm(left[0], right[1])))
+        wic_s[0:FL] = hi
+        wic_s[FL : 2 * FL] = hi
+        wic_s[2 * FL : 3 * FL] = lo
+        wic_s[3 * FL : 4 * FL] = jnp.zeros((FL, HO), BF16)
+
     ones_sea = one_where(depth[0:128] < CO)
 
     def sea_edges(row, n, r):
@@ -342,31 +391,28 @@
         st[row, pl.ds(EDGE + COLS, 3), :] = s_in[1, n, frm, :]
 
     def sea_piece(piece):
-        tops = PIECES[piece]
-        depthwise(st, taps_s, tops, 256, conv_s, 2)
-        for n, row in enumerate(tops):
-            c = conv_s[n]
-            c = c - lane_sum(c, ones_sea) * (1.0 / CO)
-            spread = lane_sum(c * c, ones_sea) * (1.0 / CO)
-            hi, lo = split(c * lax.rsqrt(spread + 1e-06))
-            pre[row] = mm_t(wi_s[...], jnp.concatenate([hi, hi], axis=1)) + mm_t(wi_s[:, 0:128], lo)
+        first, end = PIECES[piece]
+        size = (end - first) * COLS
+        c = conv_s[first:end].reshape(size, 128)
+        c = c - lane_sum(c, ones_sea, 3) * (1.0 / CO)
+        spread = lane_sum(c * c, ones_sea, 2) * (1.0 / CO)
+        hi, lo = split(c * lax.rsqrt(spread + 1e-06))
+        value = mm(jnp.concatenate([hi, lo], axis=1), wi_s[0:256]) + mm(hi, wi_s[256:384])
+        pre[first:end] = value.reshape(end - first, COLS, HO)
+
+    def sea_depthwise(tops, rows, add=False):
+        depthwise(st, taps_s, tops, rows, COLS, conv_s, 2, add)
 
     def split_weights(n):
         weight_load(n).wait()
 
         def step(b, carry):
-            w_hi[4 * n + b], w_lo[4 * n + b] = split(slots[n % 2, b].reshape(512, 128))
+            w_cat[4 * n + b, :, 0:128], w_cat[4 * n + b, :, 128:256] = split(slots[n % 2, b].reshape(512, 128))
             return carry
 
         lax.fori_loop(0, 4, step, 0)
         if n + 2 < 8:
             weight_load(n + 2).start()
-
-    for n in (2, 3):
-        sea_copies[2 + n].wait_recv()
-    for r in range(OR):
-        sea_edges(3 + r, 1, r)
-    sea_piece(0)
 
     def atm_rows(d):
         row_copies[2 * d].wait_recv()
@@ -378,12 +424,35 @@
             turn_atm(aw, ata, atb, row)
             atm_edges(row)
 
-    atm_rows(0)
+    def atm_halo(d):
+        atm_rows(d)
+        tops = tuple(range(3 - d)) + tuple(range(5 + d, AR))
+        atm_depthwise(tops, (2 - d, 11 + d), 2 if d == 0 else 4, True)
+
+    atm_depthwise((0, 1, 2, 5, 6, 7), own, 2, False)
+    split_weights(0)
+    atm_halo(0)
     atm_stage(1)
     send_own(1)
-    relay(0)
+    for c in row_copies[4:6]:
+        c.start()
     for c in sea_copies[:2]:
         c.start()
+    relay(0)
+    near_own(0)
+    sea_parameters()
+    for n in (2, 3):
+        sea_copies[2 + n].wait_recv()
+    for r in range(OR):
+        sea_edges(3 + r, 1, r)
+    sea_depthwise((3, 4, 5, 6, 7), tuple(range(3, 14)))
+    split_weights(1)
+    atm_halo(1)
+    atm_stage(2)
+    send_own(2)
+    relay(1)
+    near_relayed(0)
+    near_own(1)
 
     fold = [
         copy(20, sw.at[pl.ds(16, 3)], mirror_w, across),
@@ -398,33 +467,41 @@
         for c in fold:
             c.start()
 
-    sea_piece(1)
-    split_weights(0)
-    split_weights(1)
-    atm_rows(1)
-    atm_stage(2)
-    send_own(2)
-    relay(1)
-    forward(0, 0)
     split_weights(2)
+    far_own(0)
+    sea_depthwise((8, 9, 10, 11, 12), tuple(range(8, 19)))
+    sea_piece(0)
     split_weights(3)
-    atm_rows(2)
+    near_relayed(1)
+    far_own(1)
+    far_relayed(0)
+    atm_halo(2)
     atm_stage(3)
     send_own(3)
     relay(2)
-    forward(0, 1)
-    forward(1, 0)
     atm_store = []
     for half in range(2):
         cut = pl.ds(128 * half, 128)
         atm_store.append(pltpu.make_async_copy(back_a.at[half], atm_out.at[:, :, cut], out_sem.at[half]))
     for c in atm_store:
         c.start()
-    for n in range(4, 8):
-        split_weights(n)
+    near_own(2)
+    split_weights(4)
+    split_weights(5)
     relay(3)
-    forward(1, 1)
-    forward(2, 0)
+    split_weights(6)
+    near_own(3)
+    near_relayed(2)
+    far_own(2)
+    far_relayed(1)
+    sea_piece(1)
+    split_weights(7)
+    sea_depthwise((0, 1, 2), tuple(range(3, 9)))
+    sea_depthwise((13, 14, 15), tuple(range(13, 19)))
+    near_relayed(3)
+    far_own(3)
+    far_relayed(2)
+    far_relayed(3)
 
     for n in (0, 1, 4, 5):
         sea_copies[2 + n].wait_recv()
@@ -453,45 +530,50 @@
                 st[19 + k, pl.ds(EDGE - 3 + c, 1), :] = mirror_in[pl.ds(8 * (2 - k) + 4 + 2 - c, 1), :]
                 st[19 + k, pl.ds(EDGE + COLS + c, 1), :] = mirror_in[pl.ds(8 * (2 - k) + 2 - c, 1), :]
 
+    sea_depthwise((0, 1, 2), (0, 1, 2), True)
+    sea_depthwise((13, 14, 15), (19, 20, 21), True)
     sea_piece(2)
     sea_piece(3)
-    forward(2, 1)
-    forward(3, 0)
-    forward(3, 1)
     for stage in range(4):
         finish(stage)
 
-    def sea_row(q):
-        fluxes = []
-        for half in range(2):
-            block = 2 * q + half
-            live = count[block]
-            picked = []
-            for k in range(4):
-                index = src[k, block]
-                t, a = index // 16, lax.rem(index, 16)
-                r = a // 2
-                spot = jnp.where(r < 4, (3 - r) * 4, (r - 4) * 4 + 2) + lax.rem(a, 2)
-                picked.append(jnp.where(k < live, blocks[t, spot], 0.0))
-            hi, lo = split(jnp.concatenate(picked, axis=1))
-            both = mm(jnp.concatenate([hi, lo], axis=0), w_hi[block])
-            fluxes.append(both[0:FL] + (both[FL : 2 * FL] + mm(hi, w_lo[block])))
-        hi, lo = split(jnp.concatenate(fluxes, axis=1))
-        grown = split(gelu(pre[q] + mm(wic_s[...], jnp.concatenate([hi, lo, hi], axis=0))))
-        value = sw[3 + q] + mm_stacked(wo_s[...], CO, grown)
-        for half in range(2):
-            flat = back_s.at[half].reshape(CO * OR, 128)
-            flat[pl.ds(q, CO, stride=OR), :] = value[:, half * 128 : half * 128 + 128]
+    def flux_of(block):
+        live = count[block]
+        picked = []
+        for k in range(4):
+            index = src[k, block]
+            t, a = index // 16, lax.rem(index, 16)
+            r = a // 2
+            spot = jnp.where(r < 4, (3 - r) * 4, (r - 4) * 4 + 2) + lax.rem(a, 2)
+            picked.append(jnp.where(k < live, blocks[t, spot], 0.0))
+        hi, lo = split(jnp.concatenate(picked, axis=1))
+        both = mm(jnp.concatenate([hi, lo], axis=0), w_cat[block])
+        flux = both[0:FL, 0:128] + (both[0:FL, 128:256] + both[FL : 2 * FL, 0:128])
+        hi = flux.astype(BF16).astype(F32)
+        turned = jnp.transpose(jnp.concatenate([hi, flux - hi], axis=0)).astype(BF16)
+        return jnp.concatenate([turned, turned], axis=1)
+
+    def sea_rows(q, n):
+        flux = jnp.concatenate([flux_of(2 * q + i) for i in range(2 * n)], axis=0)
+        grown = gelu(pre[pl.ds(q, n)].reshape(n * COLS, HO) + mm(flux, wic_s[...]))
+        out = mm(jnp.concatenate(split(grown), axis=1), wo_s[...])
+        out = out[:, 0:128] + out[:, 128:256]
+        for i in range(n):
+            for half in range(2):
+                at_cell = i * COLS + half * 128
+                value = jnp.transpose(out[at_cell : at_cell + 128])[0:CO]
+                value = value + sw[3 + q + i, :, half * 128 : half * 128 + 128]
+                back_s.at[half].reshape(CO * OR, 128)[pl.ds(q + i, CO, stride=OR), :] = value
 
     sea_store = []
     for part in range(2):
 
         def step(i, carry, part=part):
-            sea_row(8 * part + 2 * i)
-            sea_row(8 * part + 2 * i + 1)
+            sea_rows(8 * part + 4 * i, 2)
+            sea_rows(8 * part + 4 * i + 2, 2)
             return carry
 
-        lax.fori_loop(0, 4, step, 0)
+        lax.fori_loop(0, 2, step, 0)
         for half in range(2):
             rows, cut = pl.ds(8 * part, 8), pl.ds(128 * half, 128)
             c = pltpu.make_async_copy(
@@ -532,21 +614,20 @@
             pltpu.VMEM((49, 8, 128), F32),
             pltpu.VMEM((49, 8, 128), F32),
             pltpu.VMEM((49, 8, 128), F32),
-            pltpu.VMEM((2, 256, 128), F32),
-            pltpu.VMEM((2, 128, 128), F32),
-            pltpu.VMEM((5, 256, 128), F32),
+            pltpu.VMEM((AR, 256, 128), F32),
+            pltpu.VMEM((AR, 128, 128), F32),
+            pltpu.VMEM((OR, 256, 128), F32),
             pltpu.VMEM((2, 3, 512, 256), BF16),
             pltpu.VMEM((2 * CA, HA), BF16),
             pltpu.VMEM((2 * FL, CA), BF16),
             pltpu.VMEM((2, HA, 2 * COLS), BF16),
-            pltpu.VMEM((HO, 256), BF16),
-            pltpu.VMEM((2 * CO, HO), BF16),
-            pltpu.VMEM((HO, 3 * FL), BF16),
-            pltpu.VMEM((OR, HO, COLS), F32),
+            pltpu.VMEM((384, HO), BF16),
+            pltpu.VMEM((2 * HO, 256), BF16),
+            pltpu.VMEM((4 * FL, HO), BF16),
+            pltpu.VMEM((OR, COLS, HO), F32),
             pltpu.VMEM((N_TILE, 16, FL, 128), F32),
             pltpu.VMEM((2, 4, 4, 128, 128), F32),
-            pltpu.VMEM((32, 512, 128), BF16),
-            pltpu.VMEM((32, 512, 128), BF16),
+            pltpu.VMEM((32, 512, 256), BF16),
             pltpu.VMEM((2, CA, AR, 128), F32),
             pltpu.VMEM((2, CO, OR, 128), F32),
             DMA((4,)),
@@ -558,20 +639,41 @@
             DMA((4, 15)),
         ],
         compiler_params=pltpu.CompilerParams(
-            collective_id=0, has_side_effects=True, vmem_limit_bytes=58 * MIB
+            collective_id=0, has_side_effects=True, vmem_limit_bytes=57 * MIB
         ),
         name="coupled",
     )(src, count, atmosphere, ocean, weights, *params)
+
+
+def hand_over_kernel(atm, sea, atm_out, sea_out):
+    atm_out[...] = atm[...]
+    sea_out[...] = sea[...]
+
+
+def hand_over(atm, sea):
+    cut = lambda channels, rows: pl.BlockSpec((channels // 4, rows, COLS), lambda i: (i, 0, 0))
+    return pl.pallas_call(
+        hand_over_kernel,
+        grid=(4,),
+        out_shape=(
+            jax.ShapeDtypeStruct((CA, AR, COLS), F32),
+            jax.ShapeDtypeStruct((CO, OR, COLS), F32),
+        ),
+        in_specs=[cut(CA, AR), cut(CO, OR)],
+        out_specs=(cut(CA, AR), cut(CO, OR)),
+        name="hand_over",
+    )(atm, sea)
 
 
 def body(
     atmosphere, ocean, kernel_atm, w_in_atm, w_out_atm, w_flux, kernel_ocean, w_in_ocean,
     w_out_ocean, w_couple, intersection_src, intersection_count, intersection_weight,
 ):
-    return step(
+    results = step(
         intersection_src[0].T, intersection_count[0], atmosphere, ocean, intersection_weight[0],
         kernel_atm.T, w_in_atm, w_out_atm, w_flux, kernel_ocean.T, w_in_ocean, w_out_ocean, w_couple.T,
     )
+    return hand_over(*results)
 
 
 def solution(mesh):

time: 125 us -> 93.9 us (0.75)
  Pallas kernels: 120 us -> 93.1 us
  local copies, waits for them, and re-layouts: 3.92 us -> 0 us
    pallas_call x1, Pallas kernels: 120 us -> 88.9 us  [step(): pl.pallas_call(fused_kernel, out_shape=(jax.ShapeDtypeStruct((CA, AR, COL...]
    pallas_call x0 -> x1, Pallas kernels: none -> 4.15 us  [hand_over(): pl.pallas_call(hand_over_kernel, grid=(4,), out_shape=(jax.ShapeDtypeStru...]
    unnamed x4 -> x0, local copies, waits for them, and re-layouts: 3.92 us -> none
where the time goes in v3:
time: 93.9 us; the launch traced here: 93.7 us
  Pallas kernels  93.1 us (99%)
    pallas_call x1, Pallas kernels, step(): pl.pallas_call(fused_kernel, out_shape=(jax.ShapeDtypeStruct((CA, AR, COL...  88.9 us
    pallas_call x1, Pallas kernels, hand_over(): pl.pallas_call(hand_over_kernel, grid=(4,), out_shape=(jax.ShapeDtypeStru...  4.15 us

profile of v3, /device:TPU:1, one launch (start us, length us, event | category | flops | bytes accessed | tf_op | source)
XLA Modules:
  0.0 93.7 jit_solution(1832595733549040840)
XLA Ops:
  0.6 88.9 %coupled.1 = (f32[192,8,256]{2,1,0:T(8,128)}, f32[96,16,256]{2,1,0:T(8,128)}) custom-call(s32[4,32]{1,0:T(4,128)} %bitcast.12, s32[32]{0:T(128)} %bitcast.13, f32[192,8,256]{2,1,0:T(8,128)} %atm_hbm.1, f32[96,16,256]{2,1,0:T(8,128)} %sea_hbm.1, f32[32,4,128,128]{3,2,1,0:T(8,128)} %bitcast.8, f32[49,192]{1,0:T(8,128)} %bitcast.9, f32[192,768]{1,0:T(8,128)} %w_in_atm.1, ...), custom_call_target="tpu_custom_call" | custom-call | tf_op jit(solution)/shard_map/coupled/pallas_call | solution.py:591
  89.6 4.1 %hand_over.1 = (f32[192,8,256]{2,1,0:T(8,128)}, f32[96,16,256]{2,1,0:T(8,128)}) custom-call(f32[192,8,256]{2,1,0:T(8,128)} %get-tuple-element.4.atm, f32[96,16,256]{2,1,0:T(8,128)} %get-tuple-element.5.sea), custom_call_target="tpu_custom_call" | custom-call | tf_op jit(solution)/shard_map/hand_over/pallas_call | solution.py:655

commit v4 on v3

--- a/solution.py
+++ b/solution.py
@@ -164,13 +164,10 @@
     loads[0].wait()
     loads[1].wait()
     rows_out_of(atm_raw, AR, CA, aw.at[pl.ds(3, AR)])
-    pl.semaphore_wait(barrier, len(near) + tile // (N_TILE - 1))
     row_copies = []
     for d in range(3):
         row_copies.append(copy(2 * d, aw.at[10 - d], aw.at[2 - d], (up, tile)))
         row_copies.append(copy(2 * d + 1, aw.at[3 + d], aw.at[11 + d], (down, tile)))
-    for c in row_copies[0:2]:
-        c.start()
 
     for r in range(AR):
         turn_atm(aw, ata, atb, 3 + r)
@@ -181,6 +178,7 @@
         to = pl.ds(16 * (r // 4) + 4 * r + 16, 3)
         a_out[0, to, :] = swap_halves(atb[3 + r, pl.ds(EDGE + 125, 3), :])
         a_out[1, to, :] = swap_halves(atb[3 + r, pl.ds(EDGE, 3), :])
+    pl.semaphore_wait(barrier, len(near) + tile // (N_TILE - 1))
     edge_copies = []
     for n, f in enumerate((up, face, down)):
         part = (pl.ds(32, 32), pl.ds(0, 64), pl.ds(0, 32))[n]
@@ -188,6 +186,8 @@
         edge_copies.append(copy(9 + n, a_out.at[1, part], a_in.at[1, n, part], (f, south)))
     for n in (2, 3, 0, 1, 4, 5):
         edge_copies[n].start()
+    for c in row_copies[0:2]:
+        c.start()
 
     def atm_edges(row):
         n = 0 if row < 3 else 1 if row < 3 + AR else 2
@@ -349,8 +349,6 @@
             c.start()
         return sea_copies
 
-    sea_copies = sea_start()
-
     for n in (2, 3):
         edge_copies[n].wait_recv()
     for r in range(AR):
@@ -359,6 +357,7 @@
     atm_depthwise((3, 4), own, 4, False)
     atm_stage(0)
     send_own(0)
+    sea_copies = sea_start()
     for c in row_copies[2:4]:
         c.start()
 
@@ -478,7 +477,6 @@
     atm_halo(2)
     atm_stage(3)
     send_own(3)
-    relay(2)
     atm_store = []
     for half in range(2):
         cut = pl.ds(128 * half, 128)
@@ -486,22 +484,19 @@
     for c in atm_store:
         c.start()
     near_own(2)
-    split_weights(4)
-    split_weights(5)
+    for n in range(4, 8):
+        split_weights(n)
+    relay(2)
+    sea_piece(1)
+    far_own(2)
+    near_relayed(2)
+    far_relayed(1)
     relay(3)
-    split_weights(6)
-    near_own(3)
-    near_relayed(2)
-    far_own(2)
-    far_relayed(1)
-    sea_piece(1)
-    split_weights(7)
     sea_depthwise((0, 1, 2), tuple(range(3, 9)))
     sea_depthwise((13, 14, 15), tuple(range(13, 19)))
-    near_relayed(3)
+    near_own(3)
     far_own(3)
     far_relayed(2)
-    far_relayed(3)
 
     for n in (0, 1, 4, 5):
         sea_copies[2 + n].wait_recv()
@@ -534,6 +529,8 @@
     sea_depthwise((13, 14, 15), (19, 20, 21), True)
     sea_piece(2)
     sea_piece(3)
+    near_relayed(3)
+    far_relayed(3)
     for stage in range(4):
         finish(stage)
 
@@ -645,22 +642,31 @@
     )(src, count, atmosphere, ocean, weights, *params)
 
 
-def hand_over_kernel(atm, sea, atm_out, sea_out):
-    atm_out[...] = atm[...]
-    sea_out[...] = sea[...]
+def hand_over_kernel(atm, sea, atm_out, sea_out, atm_here, sea_here, in_sem, out_sem):
+    loads, stores = [], []
+    for n in range(8):
+        size, frm, here, to = ((CA, atm, atm_here, atm_out), (CO, sea, sea_here, sea_out))[n % 2]
+        part = pl.ds(n // 2 * (size // 4), size // 4)
+        loads.append(pltpu.make_async_copy(frm.at[part], here.at[part], in_sem.at[n]))
+        stores.append(pltpu.make_async_copy(here.at[part], to.at[part], out_sem.at[n]))
+    for c in loads:
+        c.start()
+    for load, store in zip(loads, stores):
+        load.wait()
+        store.start()
+    for c in stores:
+        c.wait()
 
 
 def hand_over(atm, sea):
-    cut = lambda channels, rows: pl.BlockSpec((channels // 4, rows, COLS), lambda i: (i, 0, 0))
+    shapes = ((CA, AR, COLS), (CO, OR, COLS))
     return pl.pallas_call(
         hand_over_kernel,
-        grid=(4,),
-        out_shape=(
-            jax.ShapeDtypeStruct((CA, AR, COLS), F32),
-            jax.ShapeDtypeStruct((CO, OR, COLS), F32),
-        ),
-        in_specs=[cut(CA, AR), cut(CO, OR)],
-        out_specs=(cut(CA, AR), cut(CO, OR)),
+        out_shape=tuple(jax.ShapeDtypeStruct(shape, F32) for shape in shapes),
+        in_specs=[ANY, ANY],
+        out_specs=(ANY, ANY),
+        scratch_shapes=[*(pltpu.VMEM(shape, F32) for shape in shapes), DMA((8,)), DMA((8,))],
+        compiler_params=pltpu.CompilerParams(vmem_limit_bytes=58 * MIB),
         name="hand_over",
     )(atm, sea)
 

time: 93.9 us -> 87.4 us (0.931)
  the two profiles are of different devices: /device:TPU:1 before, /device:TPU:123 now
where the time goes in v4:
time: 87.4 us; the launch traced here: 87.2 us
  Pallas kernels  86.4 us (99%)
    pallas_call x1, Pallas kernels, step(): pl.pallas_call(fused_kernel, out_shape=(jax.ShapeDtypeStruct((CA, AR, COL...  83.7 us
    pallas_call x1, Pallas kernels, hand_over(): pl.pallas_call(hand_over_kernel, out_shape=tuple((jax.ShapeDtypeStruct(sh...  2.79 us

profile of v4, /device:TPU:123, one launch (start us, length us, event | category | flops | bytes accessed | tf_op | source)
XLA Modules:
  0.0 87.2 jit_solution(15883011451827313503)
XLA Ops:
  0.6 83.7 %coupled.1 = (f32[192,8,256]{2,1,0:T(8,128)}, f32[96,16,256]{2,1,0:T(8,128)}) custom-call(s32[4,32]{1,0:T(4,128)} %bitcast.12, s32[32]{0:T(128)} %bitcast.13, f32[192,8,256]{2,1,0:T(8,128)} %atm_hbm.1, f32[96,16,256]{2,1,0:T(8,128)} %sea_hbm.1, f32[32,4,128,128]{3,2,1,0:T(8,128)} %bitcast.8, f32[49,192]{1,0:T(8,128)} %bitcast.9, f32[192,768]{1,0:T(8,128)} %w_in_atm.1, ...), custom_call_target="tpu_custom_call" | custom-call | tf_op jit(solution)/shard_map/coupled/pallas_call | solution.py:588
  84.3 2.8 %hand_over.1 = (f32[192,8,256]{2,1,0:T(8,128)}, f32[96,16,256]{2,1,0:T(8,128)}) custom-call(f32[192,8,256]{2,1,0:T(8,128)} %get-tuple-element.4.atm, f32[96,16,256]{2,1,0:T(8,128)} %get-tuple-element.5.sea), custom_call_target="tpu_custom_call" | custom-call | tf_op jit(solution)/shard_map/hand_over/pallas_call | solution.py:663
